TPU v7x, 32 devices: a whole 2x2x4 slice. The times are simulated.
32 devices in a mesh: gx: 16 (over z, y, core), gy: 2 (over x).
Axes of the slice: x: 2, y: 2, z: 4, core: 2. Of those that a mesh axis runs over, the one named last changes fastest.
Arguments:
- tokens: bfloat16 [512, 6144], P('gx', 'gy'), may hold values from -30 to 30
- ln_gain: float32 [6144], P('gy'), may hold values from 0.1 to 1.9
- oft_skew: float32 [8, 24, 256, 256], P(None, 'gy'), may hold values from -0.375 to 0.375
- tenant_of_image: int32 [2], replicated, may hold values from 0 to 7
- w_qkv: bfloat16 [6144, 32, 3, 128], P('gy', 'gx'), may hold values from -0.076546554 to 0.076546554
- w_up: bfloat16 [6144, 24576], P('gy', 'gx'), may hold values from -0.078125 to 0.078125
- up_bias: float32 [24576], P('gx'), may hold values from -3 to 3
- q_gain: float32 [32, 128], P('gx'), may hold values from 0.8 to 5
- k_gain: float32 [32, 128], P('gx'), may hold values from 0.8 to 5
- w_out: bfloat16 [32, 128, 6144], P('gx', None, 'gy'), may hold values from -0.09375 to 0.09375
- w_down: bfloat16 [24576, 6144], P('gx', 'gy'), may hold values from -0.0390625 to 0.0390625
- down_bias: float32 [6144], P('gy'), may hold values from -3 to 3
Outputs:
- layer_out: bfloat16 [512, 6144], P('gx', 'gy')
All inputs are finite; a program needn't handle non-finite values.
Results may differ from a plain program's by a relative error of at most 0.005.
Values may be sent and summed in bfloat16 or wider, within the bound.
A program may use at most 128 MiB of HBM per device.

v0:
```python
import jax
import jax.numpy as jnp
from jax import lax
from jax.sharding import PartitionSpec as P

PATCHES = 256


HIGH = lax.Precision.HIGHEST


def cayley(skew_raw):
    skew_part = 0.5 * (skew_raw - jnp.swapaxes(skew_raw, -1, -2))
    identity = jnp.eye(skew_part.shape[-1], dtype=jnp.float32)
    plus_skew = identity + skew_part
    gram_matrix = identity - jnp.matmul(skew_part, skew_part, precision=HIGH)
    factor = jnp.linalg.cholesky(gram_matrix)
    lower_solved = lax.linalg.triangular_solve(factor, plus_skew, left_side=True, lower=True)
    solved = lax.linalg.triangular_solve(
        factor, lower_solved, left_side=True, lower=True, transpose_a=True
    )
    return jnp.matmul(plus_skew, solved, precision=HIGH)


def head_norm(values_in, gain):
    width_count = values_in.shape[-1]
    row_mean = jnp.sum(values_in, -1, keepdims=True) / width_count
    row_var = jnp.sum(values_in * values_in, -1, keepdims=True) / width_count - row_mean * row_mean
    return (values_in - row_mean) * lax.rsqrt(row_var + 1e-06) * gain


def per_device(
    tokens,
    ln_gain,
    oft_skew,
    tenant_of_image,
    w_qkv,
    w_up,
    up_bias,
    q_gain,
    k_gain,
    w_out,
    w_down,
    down_bias,
):
    row_count, local_width = tokens.shape
    full_width = local_width * lax.axis_size("gy")
    floats = tokens.astype(jnp.float32)
    row_sums = lax.psum((jnp.sum(floats, 1), jnp.sum(floats * floats, 1)), "gy")
    row_mean = row_sums[0][:, None] / full_width
    row_var = row_sums[1][:, None] / full_width - row_mean * row_mean
    normed = (floats - row_mean) * lax.rsqrt(row_var + 1e-06) * ln_gain
    image_index = lax.axis_index("gx") * row_count // PATCHES
    tenant = lax.dynamic_index_in_dim(tenant_of_image, image_index, 0, keepdims=False)
    skew_raw = lax.dynamic_index_in_dim(oft_skew, tenant, 0, keepdims=False)
    rotation = cayley(skew_raw)
    block_count, block_size = (skew_raw.shape[0], skew_raw.shape[1])
    turned = jnp.einsum(
        "pnb,ncb->pnc", normed.reshape(row_count, block_count, block_size), rotation, precision=HIGH
    )
    turned = turned.reshape(row_count, local_width).astype(jnp.bfloat16)
    heads_local, head_dim = (w_qkv.shape[1], w_qkv.shape[3])
    qkv_cols = heads_local * 3 * head_dim
    w_first = jnp.concatenate([w_qkv.reshape(local_width, qkv_cols), w_up], 1)
    partial_in = jnp.dot(
        lax.all_gather(turned, "gx", axis=0, tiled=True),
        w_first,
        preferred_element_type=jnp.float32,
    )
    summed = lax.psum_scatter(partial_in, "gy", scatter_dimension=0, tiled=True)
    local_tokens = summed.shape[0]
    image_count = local_tokens // PATCHES
    qkv_parts = summed[:, :qkv_cols].reshape(image_count, PATCHES, heads_local, 3, head_dim)
    queries = head_norm(qkv_parts[:, :, :, 0, :], q_gain).astype(jnp.bfloat16)
    keys_normed = head_norm(qkv_parts[:, :, :, 1, :], k_gain).astype(jnp.bfloat16)
    values = qkv_parts[:, :, :, 2, :].astype(jnp.bfloat16)
    scores = jnp.einsum(
        "iphd,iqhd->ihpq", queries, keys_normed, preferred_element_type=jnp.float32
    ) / jnp.sqrt(jnp.float32(head_dim))
    top_score = jnp.max(scores, -1, keepdims=True)
    expo = jnp.exp(scores - top_score)
    weights = (expo / jnp.sum(expo, -1, keepdims=True)).astype(jnp.bfloat16)
    attended = jnp.einsum("ihpq,iqhd->iphd", weights, values, preferred_element_type=jnp.float32)
    attended = attended.astype(jnp.bfloat16).reshape(local_tokens, heads_local * head_dim)
    hidden = jax.nn.gelu(summed[:, qkv_cols:] + up_bias, approximate=False).astype(jnp.bfloat16)
    w_attn = w_out.reshape(heads_local * head_dim, w_out.shape[2])
    partial_attn = jnp.dot(
        lax.all_gather(attended, "gy", axis=0, tiled=True),
        w_attn,
        preferred_element_type=jnp.float32,
    )
    mixed_attn = lax.psum_scatter(partial_attn, "gx", scatter_dimension=0, tiled=True)
    partial_mlp = jnp.dot(
        lax.all_gather(hidden, "gy", axis=0, tiled=True), w_down, preferred_element_type=jnp.float32
    )
    mixed_mlp = lax.psum_scatter(partial_mlp, "gx", scatter_dimension=0, tiled=True)
    mixed = mixed_attn + mixed_mlp
    return (floats + mixed + down_bias).astype(jnp.bfloat16)


def solution(mesh):
    in_specs = (
        P("gx", "gy"),
        P("gy"),
        P(None, "gy", None, None),
        P(),
        P("gy", "gx", None, None),
        P("gy", "gx"),
        P("gx"),
        P("gx", None),
        P("gx", None),
        P("gx", None, "gy"),
        P("gx", "gy"),
        P("gy"),
    )
    out_specs = P("gx", "gy")
    return jax.shard_map(
        per_device, mesh=mesh, in_specs=in_specs, out_specs=out_specs, check_vma=False
    )
```

profile of v0, /device:TPU:0, one launch (start us, length us, event | category | flops | bytes accessed | tf_op | source)
XLA Modules:
  0.0 989.0 jit_solution(16433506958368247818)
XLA Ops:
  6.5 1.4 dynamic_slice.8
  10.2 3.8 constant_dynamic-slice_fusion.1
  14.0 3.5 copy.42
  17.5 9.9 fusion.29
  27.4 3.6 copy.44
  31.0 7.3 fusion.11
  38.3 1.7 copy-done.3
  40.0 0.1 cholesky.122
  40.0 140.7 %custom-call.18 = f32[12,128,128]{2,1,0:T(8,128)S(1)} custom-call(f32[12,128,128]{2,1,0:T(8,128)S(1)} %cholesky.122), custom_call_target="Cholesky" | custom-call | tf_op jit(solution)/shard_map/jit(cholesky)/cholesky | solution.py:17
  180.7 2.0 cholesky.117
  182.7 0.1 select_bitcast_fusion
  182.8 118.7 %custom-call.19 = f32[12,1,128,128]{2,3,1,0:T(8,128)} custom-call(f32[12,1,128,128]{3,2,1,0:T(8,128)S(1)} %select_bitcast_fusion), custom_call_target="InvertDiagBlocksLowerTriangular" | custom-call | tf_op jit(solution)/shard_map/jit(cholesky)/cholesky | solution.py:17
  301.5 3.2 constant_dynamic-update-slice_fusion.1
  304.7 3.8 convolution_subtract_fusion
  308.5 141.4 %custom-call.20 = f32[12,128,128]{2,1,0:T(8,128)S(1)} custom-call(f32[12,128,128]{2,1,0:T(8,128)} %convolution_subtract_fusion), custom_call_target="Cholesky" | custom-call | tf_op jit(solution)/shard_map/jit(cholesky)/cholesky | solution.py:17
  450.0 1.1 select_reduce_fusion
  451.0 0.1 compare_reduce_fusion.1
  451.1 0.1 compare_reduce_fusion
  451.3 4.1 select_select_fusion
  455.3 0.1 triangular_solve.66
  455.4 8.4 while.1
  455.4 0.6 fusion.88
  455.9 3.8 bitcast_dynamic-update-slice_fusion.2
  459.7 0.6 fusion.88
  460.3 3.5 bitcast_dynamic-update-slice_fusion.2
  463.8 237.0 %custom-call.21 = f32[12,2,128,128]{2,3,1,0:T(8,128)S(1)} custom-call(f32[12,2,128,128]{3,2,1,0:T(8,128)} %bitcast.110), custom_call_target="InvertDiagBlocksLowerTriangular" | custom-call | tf_op jit(solution)/shard_map/triangular_solve | solution.py:19
  700.8 3.1 fusion.16
  703.9 1.5 fusion.38
  705.3 0.4 copy-done.1
  705.7 1.6 fusion.15
  707.3 1.5 fusion.35
  708.8 1.6 fusion.36
  710.4 1.5 fusion.24
  711.9 5.1 fusion.5
  717.0 0.2 convert_reduce_fusion
  717.2 5.8 all-reduce.1
  723.0 0.1 fusion.41
  723.2 4.9 fusion.31
  728.0 0.7 copy.82
  728.7 0.0 all-gather.3.cloned.1.call-update
  728.8 0.0 reduce-scatter.3.cloned.1.call-start
  728.8 12.5 %copy.53 = bf16[3072,2,3,128]{0,3,2,1:T(8,128)(2,1)} copy(bf16[3072,2,3,128]{3,1,2,0:T(2,128)(2,1)} %param.16) | data formatting | bytes 9437184 | tf_op args[4]
  741.3 6.6 copy.54
  747.9 28.0 %all-gather.3.cloned.1.call-done = bf16[512,3072]{1,0:T(8,128)(2,1)} async-done(((bf16[32,3072]{1,0:T(8,128)(2,1)}), bf16[512,3072]{1,0:T(8,128)(2,1)}) %all-gather.3.cloned.1.call-update) | async-done | bytes 3145744 | tf_op jit(solution)/shard_map/all_gather | solution.py:66
  775.9 15.6 %fusion.1 = f32[512,2304]{1,0:T(8,128)} fusion(bf16[512,3072]{1,0:T(8,128)(2,1)} %all-gather.3.cloned.1.call-done, bf16[3072,1536]{1,0:T(8,128)(2,1)} %param.17, bf16[3072,768]{1,0:T(8,128)(2,1)} %copy.54), kind=kOutput, calls=%fused_computation.3 | convolution fusion | flops 7276068864 | bytes 22020096 | tf_op jit(solution)/shard_map/dot_general | solution.py:65
  791.5 0.0 reduce-scatter.3.cloned.1.call-update
  791.6 0.0 all-gather.5.cloned.1.call-start
  791.6 58.9 %reduce-scatter.3.cloned.1.call-done = f32[256,2304]{1,0:T(8,128)} async-done(((f32[512,2304]{1,0:T(8,128)}), f32[256,2304]{1,0:T(8,128)}) %reduce-scatter.3.cloned.1.call-update) | async-done | bytes 2359312 | tf_op jit(solution)/shard_map/reduce_scatter | solution.py:70
  850.5 5.4 fusion.14
  855.9 0.0 all-gather.5.cloned.1.call-update
  856.0 0.0 reduce-scatter.5.cloned.1.call-start
  856.0 1.1 slice-done
  857.1 0.3 copy.55
  857.3 0.1 slice_reduce_fusion.1
  857.5 0.3 convolution_multiply_fusion
  857.8 0.2 fusion.70
  858.0 0.3 convolution_convert_fusion.1
  858.3 6.1 all_gather.10
  864.4 18.9 %all-gather.5.cloned.1.call-done = bf16[512,1536]{1,0:T(8,128)(2,1)} async-done(((bf16[256,1536]{1,0:T(8,128)(2,1)}), bf16[512,1536]{1,0:T(8,128)(2,1)}) %all-gather.5.cloned.1.call-update) | async-done | bytes 1572880 | tf_op jit(solution)/shard_map/all_gather | solution.py:94
  883.3 8.1 fusion.71
  891.4 3.7 convolution_add_fusion
  895.1 0.0 reduce-scatter.5.cloned.1.call-update
  895.1 85.4 %reduce-scatter.5.cloned.1.call-done = f32[32,3072]{1,0:T(8,128)} async-done(((f32[512,3072]{1,0:T(8,128)}), f32[32,3072]{1,0:T(8,128)}) %reduce-scatter.5.cloned.1.call-update) | async-done | bytes 393232 | tf_op jit(solution)/shard_map/reduce_scatter | solution.py:92
  980.5 1.7 fusion.44
  (32 shorter events, 0.2 us)
Async XLA Ops:
  6.5 884.8 %copy-start = (bf16[2,128,3072]{2,1,0:T(8,128)(2,1)S(1)}, bf16[2,128,3072]{2,1,0:T(8,128)(2,1)}, u32[]{:S(2)}) copy-start(bf16[2,128,3072]{2,1,0:T(8,128)(2,1)} %param.21) | copy-start | bytes 4718596
  6.5 769.4 %all-gather.3.cloned.1.call-start = ((), (), s32[]{:S(2)}) async-start(), calls=%async_computation.2 | async-start | bytes 3342336 | tf_op jit(solution)/shard_map/all_gather | solution.py:66
  38.3 1.7 copy-start.3
  700.8 3.1 copy-start.2
  703.9 1.9 copy-start.1
  711.9 5.1 copy-start.4
  711.9 11.1 %copy-start.5 = (f32[3072]{0:T(1024)S(1)}, f32[3072]{0:T(1024)}, u32[]{:S(2)}) copy-start(f32[3072]{0:T(1024)} %param.13) | copy-start | bytes 36868
  728.8 121.7 %reduce-scatter.3.cloned.1.call-start = ((), (), s32[]{:S(2)}) async-start(), calls=%async_computation.3 | async-start | bytes 7077888 | tf_op jit(solution)/shard_map/reduce_scatter | solution.py:70
  791.5 59.0 %copy-start.7 = (f32[1536]{0:T(1024)S(1)}, f32[1536]{0:T(1024)}, u32[]{:S(2)}) copy-start(f32[1536]{0:T(1024)} %param.18) | copy-start | bytes 18436
  791.6 91.7 %all-gather.5.cloned.1.call-start = ((), (), s32[]{:S(2)}) async-start(), calls=%async_computation.4 | async-start | bytes 2359296 | tf_op jit(solution)/shard_map/all_gather | solution.py:94
  855.9 1.2 slice-start
  855.9 1.5 copy-start.8
  855.9 1.5 copy-start.9
  856.0 124.5 %reduce-scatter.5.cloned.1.call-start = ((), (), s32[]{:S(2)}) async-start(), calls=%async_computation.5 | async-start | bytes 6684672 | tf_op jit(solution)/shard_map/reduce_scatter | solution.py:92
  895.1 85.4 %copy-start.6 = (f32[3072]{0:T(1024)S(1)}, f32[3072]{0:T(1024)}, u32[]{:S(2)}) copy-start(f32[3072]{0:T(1024)} %param.23) | copy-start | bytes 36868
Sparse Core Ops, SparseCore 0:
  728.9 46.9 all-gather.2
  791.7 58.7 reduce-scatter.2
  856.0 27.2 all-gather.4
  895.2 85.2 reduce-scatter.4
where the time goes:
time: 999 us; the launch traced here: 989 us
  other arithmetic  658 us (66%)
  waiting for transfers between devices  191 us (19%)
  matrix products  65.5 us (7%)
  local copies, waits for them, and re-layouts  46.2 us (5%)
  between operations  15.7 us (2%)
  blocking collectives  12 us (1%)
    another operation x10, other arithmetic, cayley(): factor = jnp.linalg.cholesky(gram_matrix)  402 us
    another operation x4, other arithmetic, cayley(): lax.linalg.triangular_solve(factor, lower_solved, left_side=True, lower=T...  241 us
    reduce_scatter x1, waiting for transfers between devices, per_device(): lax.psum_scatter(partial_attn, 'gx', scatter_dimension=0, tiled=True)  85.4 us
    reduce_scatter x1, waiting for transfers between devices, per_device(): summed = lax.psum_scatter(partial_in, 'gy', scatter_dimension=0, tiled=True)  58.9 us
    all_gather x1, waiting for transfers between devices, per_device(): lax.all_gather(turned, 'gx', axis=0, tiled=True)  28 us
  transfers between devices with their start and end apart: 4, of which 4 were waited for; matrix products, arithmetic and copies ran while one was open for 2% of the time, Pallas kernels for 0%

commit v1 on v0

v1 whole, which is shorter than its diff:
```python
import functools

import jax
import jax.numpy as jnp
from jax import lax
from jax.experimental import pallas as pl
from jax.experimental.pallas import tpu as pltpu
from jax.sharding import PartitionSpec as P

PATCHES = 256
HIGH = lax.Precision.HIGHEST
F32 = jnp.float32
BF16 = jnp.bfloat16


def split(a):
    high = a.astype(BF16)
    return high, (a - high.astype(F32)).astype(BF16)


def dot3(a, b):
    dot = functools.partial(jnp.dot, preferred_element_type=F32)
    return dot(a[0], b[0]) + (dot(a[0], b[1]) + dot(a[1], b[0]))


def inverse_kernel(per, tenant_ref, skew_ref, out_ref, gen_hi, gen_lo, x_ref):
    size = skew_ref.shape[-1]
    rows = lax.broadcasted_iota(jnp.int32, (size, size), 0)
    cols = lax.broadcasted_iota(jnp.int32, (size, size), 1)
    eye = (rows == cols).astype(F32)
    bound = jnp.float32(0.0)
    for k in range(per):
        raw = skew_ref[0, k]
        skew = 0.5 * (raw - raw.T)
        pair = split(skew)
        square = dot3(pair, pair)
        bound = jnp.maximum(bound, jnp.sum(square * square))
        whole = split(eye + skew)
        gen_hi[k] = whole[0]
        gen_lo[k] = whole[1]
        x_ref[k] = eye - skew
    top = 1.001 * jnp.sqrt(jnp.full((8, 128), 0.5 * bound, F32)) + 1e-3
    low = 2.0 / (2.0 + top)
    for k in range(per):
        x_ref[k] = x_ref[k] * low[0:1, 0:1]

    def more(state):
        return state[1] < 1.0 - 1e-6

    def step(state):
        low, _ = state
        grown = low * (2.0 - low)
        scale = 2.0 / (1.0 + grown)
        xs = [split(x_ref[k]) for k in range(per)]
        ys = [dot3((gen_hi[k], gen_lo[k]), xs[k]) for k in range(per)]
        rest = [split(2.0 * eye - y) for y in ys]
        for k in range(per):
            x_ref[k] = dot3(xs[k], rest[k]) * scale[0:1, 0:1]
        low = jnp.minimum(scale * grown, 1.0)
        return low, jnp.max(low)

    lax.while_loop(more, step, (low, jnp.max(low)))
    for k in range(per):
        out_ref[k] = 2.0 * x_ref[k] - eye


def turning(oft_skew, tenant):
    _, count, size, _ = oft_skew.shape
    per = next(p for p in (4, 3, 2, 1) if count % p == 0)
    return pl.pallas_call(
        functools.partial(inverse_kernel, per),
        out_shape=jax.ShapeDtypeStruct((count, size, size), F32),
        grid_spec=pltpu.PrefetchScalarGridSpec(
            num_scalar_prefetch=1,
            grid=(count // per,),
            in_specs=[pl.BlockSpec((1, per, size, size), lambda i, t: (t[0], i, 0, 0))],
            out_specs=pl.BlockSpec((per, size, size), lambda i, t: (i, 0, 0)),
            scratch_shapes=[
                pltpu.VMEM((per, size, size), BF16),
                pltpu.VMEM((per, size, size), BF16),
                pltpu.VMEM((per, size, size), F32),
            ],
        ),
        compiler_params=pltpu.CompilerParams(vmem_limit_bytes=32 * 2**20),
        cost_estimate=pl.CostEstimate(flops=count * 50 * 2 * size**3, bytes_accessed=count * 8 * size**2, transcendentals=0),
    )(tenant.reshape(1), oft_skew)


def lay_kernel(ways, w_ref, out_ref):
    block = 64
    size = ways * block
    rows = lax.broadcasted_iota(jnp.int32, (size, size), 0)
    cols = lax.broadcasted_iota(jnp.int32, (size, size), 1)
    move = (cols == (rows % block) * ways + rows // block).astype(BF16)
    for k in range(out_ref.shape[0] // block):
        laid = jnp.dot(move, w_ref[k * size : (k + 1) * size, :], preferred_element_type=F32).astype(BF16)
        for c in range(ways):
            out_ref[k * block : (k + 1) * block, c * 128 : (c + 1) * 128] = laid[c * block : (c + 1) * block, :]


def lay_qkv(w_qkv):
    depth, heads, three, dim = w_qkv.shape
    ways = heads * three
    turned = w_qkv.transpose(0, 2, 1, 3)
    if heads != 2 or dim != 128 or depth % 512:
        return turned.reshape(depth, ways * dim)
    return pl.pallas_call(
        functools.partial(lay_kernel, ways),
        out_shape=jax.ShapeDtypeStruct((depth, ways * dim), BF16),
        grid=(depth // 512,),
        in_specs=[pl.BlockSpec((512 * ways, dim), lambda i: (i, 0))],
        out_specs=pl.BlockSpec((512, ways * dim), lambda i: (i, 0)),
        cost_estimate=pl.CostEstimate(flops=2 * depth * ways * dim * 384, bytes_accessed=4 * depth * ways * dim, transcendentals=0),
    )(turned.reshape(depth * ways, dim))


def head_norm(values_in, gain):
    width_count = values_in.shape[-1]
    row_mean = jnp.sum(values_in, -1, keepdims=True) / width_count
    row_var = jnp.sum(values_in * values_in, -1, keepdims=True) / width_count - row_mean * row_mean
    return (values_in - row_mean) * lax.rsqrt(row_var + 1e-06) * gain


def attention(qkv, q_gain, k_gain):
    heads, dim = q_gain.shape
    count = qkv.shape[0] // PATCHES
    parts = qkv.reshape(count, PATCHES, 3, heads, dim)
    queries = head_norm(parts[:, :, 0], q_gain).astype(BF16)
    keys_normed = head_norm(parts[:, :, 1], k_gain).astype(BF16)
    values = parts[:, :, 2].astype(BF16)
    scores = jnp.einsum("iphd,iqhd->ihpq", queries, keys_normed, preferred_element_type=F32) / jnp.sqrt(F32(dim))
    expo = jnp.exp(scores - jnp.max(scores, -1, keepdims=True))
    weights = (expo / jnp.sum(expo, -1, keepdims=True)).astype(BF16)
    attended = jnp.einsum("ihpq,iqhd->iphd", weights, values, preferred_element_type=F32)
    return attended.astype(BF16).reshape(-1, heads * dim)


def per_device(
    tokens, ln_gain, oft_skew, tenant_of_image, w_qkv, w_up, up_bias, q_gain, k_gain, w_out, w_down, down_bias
):
    row_count, local_width = tokens.shape
    ways = lax.axis_size("gy")
    full_width = local_width * ways
    gx, gy = lax.axis_index("gx"), lax.axis_index("gy")
    dot = functools.partial(jnp.dot, preferred_element_type=F32)

    tenant = lax.dynamic_index_in_dim(tenant_of_image, gx * row_count // PATCHES, 0, keepdims=False)
    rotation = turning(oft_skew, tenant)
    floats = tokens.astype(F32)
    sums = jnp.stack([jnp.sum(floats, 1), jnp.sum(floats * floats, 1)])
    if ways == 2:
        swap = functools.partial(lax.ppermute, axis_name="gy", perm=[(0, 1), (1, 0)])
        sums = sums + swap(sums)
    else:
        sums = lax.psum(sums, "gy")
    row_mean = sums[0][:, None] / full_width
    row_var = sums[1][:, None] / full_width - row_mean * row_mean
    normed = (floats - row_mean) * lax.rsqrt(row_var + 1e-06) * ln_gain
    count, size = rotation.shape[:2]
    turned = jnp.einsum("pnb,nbc->pnc", normed.reshape(row_count, count, size), rotation, precision=HIGH)
    turned = turned.reshape(row_count, local_width).astype(BF16)
    w_first = lay_qkv(w_qkv)
    every = lax.all_gather(turned, "gx", axis=0, tiled=True)

    qkv_cols, up_cols = w_first.shape[1], w_up.shape[1]
    w_attn = w_out.reshape(-1, w_out.shape[2])
    if ways == 2:
        half = every.shape[0] // 2
        mine = lax.dynamic_slice_in_dim(every, gy * half, half, 0)
        theirs = lax.dynamic_slice_in_dim(every, (1 - gy) * half, half, 0)
        cut = up_cols // 3
        pieces = [w_first] + [w_up[:, k * cut : (k + 1) * cut] for k in range(3)]
        got = [swap(dot(theirs, w).astype(BF16)) for w in pieces]
        own = [dot(mine, w) for w in pieces]
        summed = [a + b.astype(F32) for a, b in zip(own, got)]
        acts = [attention(summed[0], q_gain, k_gain)]
        for k in range(3):
            pre = summed[k + 1] + up_bias[k * cut : (k + 1) * cut]
            acts.append(jax.nn.gelu(pre, approximate=False).astype(BF16))
        others = [swap(a) for a in acts]
        mixed_own = dot(acts[0], w_attn) + dot(jnp.concatenate(acts[1:], 1), w_down)
        mixed_other = dot(others[0], w_attn) + dot(jnp.concatenate(others[1:], 1), w_down)
        mixed_own, mixed_other = mixed_own.astype(BF16), mixed_other.astype(BF16)
        first = gy == 0
        mixed = jnp.concatenate(
            [jnp.where(first, mixed_own, mixed_other), jnp.where(first, mixed_other, mixed_own)], 0
        )
    else:
        part = jnp.concatenate([dot(every, w_first), dot(every, w_up)], 1)
        summed = lax.psum_scatter(part.astype(BF16), "gy", scatter_dimension=0, tiled=True).astype(F32)
        acts = jnp.concatenate(
            [
                attention(summed[:, :qkv_cols], q_gain, k_gain),
                jax.nn.gelu(summed[:, qkv_cols:] + up_bias, approximate=False).astype(BF16),
            ],
            1,
        )
        acts = lax.all_gather(acts, "gy", axis=0, tiled=True)
        heads_cols = w_attn.shape[0]
        mixed = (dot(acts[:, :heads_cols], w_attn) + dot(acts[:, heads_cols:], w_down)).astype(BF16)
    mixed = lax.psum_scatter(mixed, "gx", scatter_dimension=0, tiled=True)
    return (floats + mixed.astype(F32) + down_bias).astype(BF16)


def solution(mesh):
    in_specs = (
        P("gx", "gy"),
        P("gy"),
        P(None, "gy", None, None),
        P(),
        P("gy", "gx", None, None),
        P("gy", "gx"),
        P("gx"),
        P("gx", None),
        P("gx", None),
        P("gx", None, "gy"),
        P("gx", "gy"),
        P("gy"),
    )
    return jax.shard_map(per_device, mesh=mesh, in_specs=in_specs, out_specs=P("gx", "gy"), check_vma=False)
```

time: 999 us -> 221 us (0.22)
  other arithmetic: 658 us -> 5.91 us
  waiting for transfers between devices: 191 us -> 109 us
  local copies, waits for them, and re-layouts: 46.2 us -> 4.13 us
  Pallas kernels: 0 us -> 37.5 us
  matrix products: 65.5 us -> 39.2 us
  blocking collectives: 12 us -> 0 us
  starting transfers between devices: 0.13 us -> 11.6 us
    another operation x14 -> x1, other arithmetic: 643 us -> 0.01 us  [per_device(): sums = jnp.stack([jnp.sum(floats, 1), jnp.sum(floats * floats, 1)])]
    reduce_scatter x2 -> x1, waiting for transfers between devices: 144 us -> 65.2 us  [per_device(): mixed = lax.psum_scatter(mixed, 'gx', scatter_dimension=0, tiled=True)]
    pallas_call x0 -> x2, Pallas kernels: none -> 37.5 us  [the longest x1 29.3 us: turning(): pl.pallas_call(functools.partial(inverse_kernel, per), out_shape=jax.Shap...]
    another operation x8 -> x0, matrix products: 17.7 us -> none  [the longest x2 7.03 us: cayley(): factor = jnp.linalg.cholesky(gram_matrix)]
    unnamed x21 -> x35, local copies, waits for them, and re-layouts: 14.6 us -> 0.34 us
    ppermute x0 -> x9, starting transfers between devices: none -> 11.6 us  [the longest x4 4.46 us: per_device(): got = [swap(dot(theirs, w).astype(BF16)) for w in pieces]]
    another operation x9 -> x0, local copies, waits for them, and re-layouts: 10.5 us -> none
    all_gather x2 -> x1, waiting for transfers between devices: 46.9 us -> 37.4 us  [per_device(): every = lax.all_gather(turned, 'gx', axis=0, tiled=True)]
  transfers between devices with their start and end apart: 4 -> 11, of which waited for: 4 -> 5; matrix products, arithmetic and copies ran while one was open for 2% -> 17% of each run, Pallas kernels for 0% -> 17%
where the time goes in v1:
time: 221 us
  waiting for transfers between devices  109 us (49%)
  matrix products  39.2 us (18%)
  Pallas kernels  37.5 us (17%)
  between operations  13.7 us (6%)
  starting transfers between devices  11.6 us (5%)
  other arithmetic  5.91 us (3%)
  local copies, waits for them, and re-layouts  4.13 us (2%)
    reduce_scatter x1, waiting for transfers between devices, per_device(): mixed = lax.psum_scatter(mixed, 'gx', scatter_dimension=0, tiled=True)  65.2 us
    all_gather x1, waiting for transfers between devices, per_device(): every = lax.all_gather(turned, 'gx', axis=0, tiled=True)  37.4 us
    pallas_call x1, Pallas kernels, turning(): pl.pallas_call(functools.partial(inverse_kernel, per), out_shape=jax.Shap...  29.3 us
    dot_general x4, matrix products, per_device(): got = [swap(dot(theirs, w).astype(BF16)) for w in pieces]  11.5 us
    dot_general x4, matrix products, per_device(): own = [dot(mine, w) for w in pieces]  10.7 us
    pallas_call x1, Pallas kernels, lay_qkv(): pl.pallas_call(functools.partial(lay_kernel, ways), out_shape=jax.ShapeDt...  8.21 us
    dot_general x2, matrix products, per_device(): mixed_own = dot(acts[0], w_attn) + dot(jnp.concatenate(acts[1:], 1), w_down)  7.86 us
    ppermute x4, waiting for transfers between devices, per_device(): others = [swap(a) for a in acts]  6.09 us
  transfers between devices with their start and end apart: 11, of which 5 were waited for; matrix products, arithmetic and copies ran while one was open for 17% of the time, Pallas kernels for 17%

profile of v1, /device:TPU:0, one launch (start us, length us, event | category | flops | bytes accessed | tf_op | source)
XLA Modules:
  0.0 220.9 jit_solution(10774898142413443735)
XLA Ops:
  6.5 0.0 copy-start
  6.5 1.2 convert_reduce_fusion
  7.8 3.0 %collective-permute-start = (f32[2,32]{1,0:T(2,128)S(1)}, f32[2,32]{1,0:T(2,128)S(1)}, u32[]{:S(2)}, u32[]{:S(2)}) collective-permute-start(f32[2,32]{1,0:T(2,128)S(1)} %pad_maximum_fusion.1), channel_id=1, source_target_pairs={{0,1},{1,0},{2,3},{3,2},{4,5},{5,4},{6,7},{7,6},{8,9},{9,8},{10,11... | collective-permute-start | bytes 776 | tf_op jit(solution)/shard_map/ppermute | solution.py:153
  10.8 1.2 dynamic_slice.10.tenant_ref
  12.0 29.3 %shard_map.118 = f32[12,256,256]{2,1,0:T(8,128)S(1)} custom-call(s32[1]{0:T(128)} %dynamic_slice.10.tenant_ref, f32[8,12,256,256]{3,2,1,0:T(8,128)} %skew_ref.1), custom_call_target="tpu_custom_call" | custom-call | flops 20132659200 | bytes 6291456 | tf_op jit(solution)/shard_map/pallas_call | solution.py:70
  41.3 0.0 collective-permute-done
  41.3 0.0 copy-done.1
  41.3 0.0 copy-done.2
  41.4 0.1 fusion.80
  41.5 2.0 fusion.26
  43.5 0.7 copy.31
  44.2 0.0 all-gather.2.cloned.1.call-update
  44.2 0.0 reduce-scatter.2.cloned.1.call-start
  44.3 0.0 copy-start.4
  44.3 8.2 %shard_map.119 = bf16[3072,768]{1,0:T(8,128)(2,1)} custom-call(bf16[18432,128]{1,0:T(8,128)(2,1)} %bitcast.63), custom_call_target="tpu_custom_call" | custom-call | flops 1811939328 | bytes 9437184 | tf_op jit(solution)/shard_map/pallas_call | solution.py:107
  52.5 0.0 copy-done.4
  52.5 37.4 %all-gather.2.cloned.1.call-done = bf16[512,3072]{1,0:T(8,128)(2,1)} async-done(((bf16[32,3072]{1,0:T(8,128)(2,1)}), bf16[512,3072]{1,0:T(8,128)(2,1)}) %all-gather.2.cloned.1.call-update) | async-done | bytes 3145744 | tf_op jit(solution)/shard_map/all_gather | solution.py:163
  89.9 3.5 %fusion.17 = bf16[256,512]{1,0:T(8,128)(2,1)S(1)} fusion(bf16[3072,1536]{1,0:T(8,128)(2,1)} %param.17, bf16[512,3072]{1,0:T(8,128)(2,1)} %all-gather.2.cloned.1.call-done, s32[]{:T(128)S(6)} %select_n.31), kind=kOutput, calls=%fused_computation.24 | convolution fusion | flops 805437440 | bytes 4980740 | tf_op jit(solution)/shard_map/dot_general | solution.py:173
  93.4 0.0 slice-start.1
  93.4 1.5 collective-permute-start.2
  94.9 3.5 %fusion.20 = bf16[256,512]{1,0:T(8,128)(2,1)S(1)} fusion(bf16[3072,1536]{1,0:T(8,128)(2,1)} %param.17, bf16[512,3072]{1,0:T(8,128)(2,1)} %all-gather.2.cloned.1.call-done, s32[]{:T(128)S(6)} %select_n.31), kind=kOutput, calls=%fused_computation.25 | convolution fusion | flops 805437440 | bytes 4980740 | tf_op jit(solution)/shard_map/dot_general | solution.py:173
  98.4 0.0 slice-start.3
  98.4 0.8 collective-permute-start.3
  99.2 3.2 %fusion.23 = bf16[256,512]{1,0:T(8,128)(2,1)S(1)} fusion(bf16[3072,1536]{1,0:T(8,128)(2,1)} %param.17, bf16[512,3072]{1,0:T(8,128)(2,1)S(1)} %copy-done.7, s32[]{:T(128)S(6)} %select_n.31), kind=kOutput, calls=%fused_computation.26 | convolution fusion | flops 805437440 | bytes 4980740 | tf_op jit(solution)/shard_map/dot_general | solution.py:173
  102.4 0.0 slice-start.4
  102.4 1.1 collective-permute-start.4
  103.5 0.0 slice-done
  103.5 1.4 convolution_convert_fusion
  104.9 1.1 collective-permute-start.1
  106.0 0.0 collective-permute-done.2
  106.0 2.8 %fusion.50 = bf16[256,512]{1,0:T(8,128)(2,1)} fusion(bf16[256,512]{1,0:T(8,128)(2,1)S(1)} %collective-permute-done.2, f32[512]{0:T(512)S(1)} %get-tuple-element.13, bf16[3072,1536]{1,0:T(8,128)(2,1)S(1)} %bitcast.75, bf16[512,3072]{1,0:T(8,128)(2,1)S(1)} %copy-done.7, s32[]{:T(128)S(6)} %select_n.30), kind=kOutput, calls=%fused_computation.61 | convolution fusion | flops 814219264 | bytes 5244932 | tf_op jit(solution)/shard_map/dot_general | solution.py:174
  108.8 1.0 collective-permute-start.6
  109.8 0.0 collective-permute-done.3
  109.8 2.8 %fusion.53 = bf16[256,512]{1,0:T(8,128)(2,1)} fusion(bf16[256,512]{1,0:T(8,128)(2,1)S(1)} %collective-permute-done.3, f32[512]{0:T(512)S(1)} %get-tuple-element.15, bf16[3072,1536]{1,0:T(8,128)(2,1)S(1)} %bitcast.75, bf16[512,3072]{1,0:T(8,128)(2,1)S(1)} %copy-done.7, s32[]{:T(128)S(6)} %select_n.30), kind=kOutput, calls=%fused_computation.64 | convolution fusion | flops 814219264 | bytes 5244932 | tf_op jit(solution)/shard_map/dot_general | solution.py:174
  112.6 1.0 collective-permute-start.7
  113.6 0.2 collective-permute-done.4
  113.8 2.8 %fusion.56 = bf16[256,512]{1,0:T(8,128)(2,1)} fusion(bf16[256,512]{1,0:T(8,128)(2,1)S(1)} %collective-permute-done.4, f32[512]{0:T(512)S(1)} %get-tuple-element.14, bf16[3072,1536]{1,0:T(8,128)(2,1)S(1)} %bitcast.75, bf16[512,3072]{1,0:T(8,128)(2,1)S(1)} %copy-done.7, s32[]{:T(128)S(6)} %select_n.30), kind=kOutput, calls=%fused_computation.67 | convolution fusion | flops 814219264 | bytes 5244932 | tf_op jit(solution)/shard_map/dot_general | solution.py:174
  116.6 1.5 collective-permute-start.8
  118.1 0.0 slice-done.7
  118.1 5.4 %fusion.36 = f32[256,3072]{1,0:T(8,128)} fusion(bf16[1536,3072]{1,0:T(8,128)(2,1)S(1)} %bitcast.77, bf16[256,512]{1,0:T(8,128)(2,1)} %fusion.56, bf16[256,512]{1,0:T(8,128)(2,1)} %fusion.53, bf16[256,512]{1,0:T(8,128)(2,1)} %fusion.50), kind=kOutput, calls=%fused_computation.39 | convolution fusion | flops 2418278400 | bytes 13369344 | tf_op jit(solution)/shard_map/dot_general | solution.py:181
  123.5 0.0 collective-permute-done.1
  123.5 2.3 %convert_add_fusion = f32[256,768]{1,0:T(8,128)} fusion(bf16[256,768]{1,0:T(8,128)(2,1)S(1)} %collective-permute-done.1, bf16[3072,768]{1,0:T(8,128)(2,1)S(1)} %bitcast.65, bf16[512,3072]{1,0:T(8,128)(2,1)S(1)} %copy-done.7, s32[]{:T(128)S(6)} %select_n.30), kind=kOutput, calls=%fused_computation.54 | convolution fusion | flops 1208352768 | bytes 7471108 | tf_op jit(solution)/shard_map/dot_general | solution.py:174
  125.8 1.8 reshape.186
  127.6 0.6 slice_reduce_fusion.1
  128.2 0.1 slice.45
  128.3 0.1 copy.27
  128.4 0.1 copy.28
  128.5 0.2 multiply_reduce_fusion
  128.7 0.7 convolution_multiply_fusion
  129.5 0.2 fusion.130
  129.6 0.1 copy.29
  129.7 0.3 convolution_convert_fusion.2
  130.0 0.6 collective-permute-start.5
  130.6 2.5 %fusion.1 = bf16[256,3072]{1,0:T(8,128)(2,1)S(1)} fusion(f32[256,3072]{1,0:T(8,128)} %fusion.36, bf16[256,256]{0,1:T(8,128)(2,1)S(1)} %bitcast.69, bf16[256,3072]{1,0:T(8,128)(2,1)S(1)} %bitcast.61), kind=kOutput, calls=%fused_computation.3 | convolution fusion | flops 404226048 | bytes 6422528 | tf_op jit(solution)/shard_map/dot_general | solution.py:181
  133.1 0.0 collective-permute-done.6
  133.1 0.5 collective-permute-done.7
  133.6 5.6 %collective-permute-done.8 = bf16[256,512]{1,0:T(8,128)(2,1)} collective-permute-done((bf16[256,512]{1,0:T(8,128)(2,1)}, bf16[256,512]{1,0:T(8,128)(2,1)}, u32[]{:S(2)}, u32[]{:S(2)}) %collective-permute-start.8) | collective-permute-done | bytes 262176 | tf_op jit(solution)/shard_map/ppermute | solution.py:180
  139.2 5.4 %fusion.42 = f32[256,3072]{1,0:T(8,128)S(1)} fusion(bf16[1536,3072]{1,0:T(8,128)(2,1)} %param.22, bf16[256,512]{1,0:T(8,128)(2,1)} %collective-permute-done.8, bf16[256,512]{1,0:T(8,128)(2,1)} %collective-permute-done.7, bf16[256,512]{1,0:T(8,128)(2,1)} %collective-permute-done.6), kind=kOutput, calls=%fused_computation.45 | convolution fusion | flops 2418278400 | bytes 13369344 | tf_op jit(solution)/shard_map/dot_general | solution.py:182
  144.6 0.0 collective-permute-done.5
  144.7 0.7 broadcast_select_fusion.1
  145.3 1.9 pad_maximum_fusion
  147.2 0.0 reduce-scatter.2.cloned.1.call-update
  147.2 65.2 %reduce-scatter.2.cloned.1.call-done = bf16[32,3072]{1,0:T(8,128)(2,1)} async-done(((bf16[512,3072]{1,0:T(8,128)(2,1)}), bf16[32,3072]{1,0:T(8,128)(2,1)}) %reduce-scatter.2.cloned.1.call-update) | async-done | bytes 196624 | tf_op jit(solution)/shard_map/reduce_scatter | solution.py:201
  212.4 1.7 fusion.82
  (33 shorter events, 0.1 us)
Async XLA Ops:
  6.5 124.1 %copy-start = (bf16[2,128,3072]{2,1,0:T(8,128)(2,1)S(1)}, bf16[2,128,3072]{2,1,0:T(8,128)(2,1)}, u32[]{:S(2)}) copy-start(bf16[2,128,3072]{2,1,0:T(8,128)(2,1)} %param.21) | copy-start | bytes 4718596
  6.5 83.3 %all-gather.2.cloned.1.call-start = ((), (), s32[]{:S(2)}) async-start(), calls=%async_computation.1 | async-start | bytes 3342336 | tf_op jit(solution)/shard_map/all_gather | solution.py:163
  7.8 33.5 %collective-permute-start = (f32[2,32]{1,0:T(2,128)S(1)}, f32[2,32]{1,0:T(2,128)S(1)}, u32[]{:S(2)}, u32[]{:S(2)}) collective-permute-start(f32[2,32]{1,0:T(2,128)S(1)} %pad_maximum_fusion.1), channel_id=1, source_target_pairs={{0,1},{1,0},{2,3},{3,2},{4,5},{5,4},{6,7},{7,6},{8,9},{9,8},{10,11... | collective-permute-start | bytes 776 | tf_op jit(solution)/shard_map/ppermute | solution.py:153
  12.0 29.3 %copy-start.1 = (bf16[32,3072]{1,0:T(8,128)(2,1)S(1)}, bf16[32,3072]{1,0:T(8,128)(2,1)}, u32[]{:S(2)}) copy-start(bf16[32,3072]{1,0:T(8,128)(2,1)} %param.12) | copy-start | bytes 589828
  12.0 29.3 %copy-start.2 = (f32[3072]{0:T(1024)S(1)}, f32[3072]{0:T(1024)}, u32[]{:S(2)}) copy-start(f32[3072]{0:T(1024)} %param.13) | copy-start | bytes 36868
  44.2 168.2 %reduce-scatter.2.cloned.1.call-start = ((), (), s32[]{:S(2)}) async-start(), calls=%async_computation.2 | async-start | bytes 3342336 | tf_op jit(solution)/shard_map/reduce_scatter | solution.py:201
  44.3 8.2 %copy-start.4 = (f32[1536]{0:T(1024)S(1)}, f32[1536]{0:T(1024)}, u32[]{:S(2)}) copy-start(f32[1536]{0:T(1024)} %param.18) | copy-start | bytes 18436
  89.9 13.6 %slice-start = ((s8[4718592]{0:T(1024)(128)(4,1)}), s8[4194304]{0:T(1024)(128)(4,1)S(1)}, s32[]{:S(2)}) async-start(s8[4718592]{0:T(1024)(128)(4,1)} %bitcast.64), calls=%async_computation.3 | async-start | bytes 8388608
  93.4 5.8 %copy-start.7 = (bf16[512,3072]{1,0:T(8,128)(2,1)S(1)}, bf16[512,3072]{1,0:T(8,128)(2,1)}, u32[]{:S(2)}) copy-start(bf16[512,3072]{1,0:T(8,128)(2,1)} %all-gather.2.cloned.1.call-done) | copy-start | bytes 9437188
  93.4 10.1 %slice-start.1 = ((s8[4718592]{0:T(1024)(128)(4,1)}), s8[524288]{0:T(1024)(128)(4,1)S(1)}, s32[]{:S(2)}) async-start(s8[4718592]{0:T(1024)(128)(4,1)} %bitcast.64), calls=%async_computation.4 | async-start | bytes 1048576
  93.4 12.6 %collective-permute-start.2 = (bf16[256,512]{1,0:T(8,128)(2,1)S(1)}, bf16[256,512]{1,0:T(8,128)(2,1)S(1)}, u32[]{:S(2)}, u32[]{:S(2)}) collective-permute-start(bf16[256,512]{1,0:T(8,128)(2,1)S(1)} %fusion.17), channel_id=1, source_target_pairs={{0,1},{1,0},{2,3},{3,2},{4,5},{5,4},{6,7},{7,6},{8,9},{9,8},{10,11... | collective-permute-start | bytes 786440 | tf_op jit(solution)/shard_map/ppermute | solution.py:173
  94.9 11.0 %slice-start.2 = ((s8[9437184]{0:T(1024)(128)(4,1)}), s8[4194304]{0:T(1024)(128)(4,1)S(1)}, s32[]{:S(2)}) async-start(s8[9437184]{0:T(1024)(128)(4,1)} %bitcast.74), calls=%async_computation.5 | async-start | bytes 8388608
  98.4 7.6 %slice-start.3 = ((s8[9437184]{0:T(1024)(128)(4,1)}), s8[4194304]{0:T(1024)(128)(4,1)S(1)}, s32[]{:S(2)}) async-start(s8[9437184]{0:T(1024)(128)(4,1)} %bitcast.74), calls=%async_computation.6 | async-start | bytes 8388608
  98.4 11.4 %collective-permute-start.3 = (bf16[256,512]{1,0:T(8,128)(2,1)S(1)}, bf16[256,512]{1,0:T(8,128)(2,1)S(1)}, u32[]{:S(2)}, u32[]{:S(2)}) collective-permute-start(bf16[256,512]{1,0:T(8,128)(2,1)S(1)} %fusion.20), channel_id=1, source_target_pairs={{0,1},{1,0},{2,3},{3,2},{4,5},{5,4},{6,7},{7,6},{8,9},{9,8},{10,11... | collective-permute-start | bytes 786440 | tf_op jit(solution)/shard_map/ppermute | solution.py:173
  102.4 3.6 %slice-start.4 = ((s8[9437184]{0:T(1024)(128)(4,1)}), s8[1048576]{0:T(1024)(128)(4,1)S(1)}, s32[]{:S(2)}) async-start(s8[9437184]{0:T(1024)(128)(4,1)} %bitcast.74), calls=%async_computation.7 | async-start | bytes 2097152
  102.4 11.4 %collective-permute-start.4 = (bf16[256,512]{1,0:T(8,128)(2,1)S(1)}, bf16[256,512]{1,0:T(8,128)(2,1)S(1)}, u32[]{:S(2)}, u32[]{:S(2)}) collective-permute-start(bf16[256,512]{1,0:T(8,128)(2,1)S(1)} %fusion.23), channel_id=1, source_target_pairs={{0,1},{1,0},{2,3},{3,2},{4,5},{5,4},{6,7},{7,6},{8,9},{9,8},{10,11... | collective-permute-start | bytes 786440 | tf_op jit(solution)/shard_map/ppermute | solution.py:173
  104.9 18.6 %collective-permute-start.1 = (bf16[256,768]{1,0:T(8,128)(2,1)S(1)}, bf16[256,768]{1,0:T(8,128)(2,1)S(1)}, u32[]{:S(2)}, u32[]{:S(2)}) collective-permute-start(bf16[256,768]{1,0:T(8,128)(2,1)S(1)} %convolution_convert_fusion), channel_id=1, source_target_pairs={{0,1},{1,0},{2,3},{3,2},{4,5},{5,4},{6,7},{7,6},{8,9},{9,8},{10,11... | collective-permute-start | bytes 1179656 | tf_op jit(solution)/shard_map/ppermute | solution.py:173
  108.8 24.3 %collective-permute-start.6 = (bf16[256,512]{1,0:T(8,128)(2,1)}, bf16[256,512]{1,0:T(8,128)(2,1)}, u32[]{:S(2)}, u32[]{:S(2)}) collective-permute-start(bf16[256,512]{1,0:T(8,128)(2,1)} %fusion.50), channel_id=1, source_target_pairs={{0,1},{1,0},{2,3},{3,2},{4,5},{5,4},{6,7},{7,6},{8,9},{9,8},{10,11... | collective-permute-start | bytes 786440 | tf_op jit(solution)/shard_map/ppermute | solution.py:180
  109.8 8.3 %slice-start.5 = ((s8[9437184]{0:T(1024)(128)(4,1)}), s8[4194304]{0:T(1024)(128)(4,1)S(1)}, s32[]{:S(2)}) async-start(s8[9437184]{0:T(1024)(128)(4,1)} %bitcast.76), calls=%async_computation.8 | async-start | bytes 8388608
  109.8 8.3 %slice-start.6 = ((s8[9437184]{0:T(1024)(128)(4,1)}), s8[4194304]{0:T(1024)(128)(4,1)S(1)}, s32[]{:S(2)}) async-start(s8[9437184]{0:T(1024)(128)(4,1)} %bitcast.76), calls=%async_computation.9 | async-start | bytes 8388608
  112.6 21.0 %collective-permute-start.7 = (bf16[256,512]{1,0:T(8,128)(2,1)}, bf16[256,512]{1,0:T(8,128)(2,1)}, u32[]{:S(2)}, u32[]{:S(2)}) collective-permute-start(bf16[256,512]{1,0:T(8,128)(2,1)} %fusion.53), channel_id=1, source_target_pairs={{0,1},{1,0},{2,3},{3,2},{4,5},{5,4},{6,7},{7,6},{8,9},{9,8},{10,11... | collective-permute-start | bytes 786440 | tf_op jit(solution)/shard_map/ppermute | solution.py:180
  113.8 4.3 %slice-start.7 = ((s8[9437184]{0:T(1024)(128)(4,1)}), s8[1048576]{0:T(1024)(128)(4,1)S(1)}, s32[]{:S(2)}) async-start(s8[9437184]{0:T(1024)(128)(4,1)} %bitcast.76), calls=%async_computation.10 | async-start | bytes 2097152
  116.6 22.6 %collective-permute-start.8 = (bf16[256,512]{1,0:T(8,128)(2,1)}, bf16[256,512]{1,0:T(8,128)(2,1)}, u32[]{:S(2)}, u32[]{:S(2)}) collective-permute-start(bf16[256,512]{1,0:T(8,128)(2,1)} %fusion.56), channel_id=1, source_target_pairs={{0,1},{1,0},{2,3},{3,2},{4,5},{5,4},{6,7},{7,6},{8,9},{9,8},{10,11... | collective-permute-start | bytes 786440 | tf_op jit(solution)/shard_map/ppermute | solution.py:180
  125.8 2.9 %copy-start.5 = (f32[2,128]{1,0:T(2,128)S(1)}, f32[2,128]{1,0:T(2,128)}, u32[]{:S(2)}) copy-start(f32[2,128]{1,0:T(2,128)} %param.20) | copy-start | bytes 3076
  125.8 2.9 %copy-start.6 = (f32[2,128]{1,0:T(2,128)S(1)}, f32[2,128]{1,0:T(2,128)}, u32[]{:S(2)}) copy-start(f32[2,128]{1,0:T(2,128)} %param.19) | copy-start | bytes 3076
  130.0 14.6 %collective-permute-start.5 = (bf16[256,256]{0,1:T(8,128)(2,1)S(1)}, bf16[256,256]{0,1:T(8,128)(2,1)S(1)}, u32[]{:S(2)}, u32[]{:S(2)}) collective-permute-start(bf16[256,256]{0,1:T(8,128)(2,1)S(1)} %bitcast.68), channel_id=1, source_target_pairs={{0,1},{1,0},{2,3},{3,2},{4,5},{5,4},{6,7},{7,6},{8,9},{9,8},{10,11... | collective-permute-start | bytes 393224 | tf_op jit(solution)/shard_map/ppermute | solution.py:180
  147.2 65.2 %copy-start.3 = (f32[3072]{0:T(1024)S(1)}, f32[3072]{0:T(1024)}, u32[]{:S(2)}) copy-start(f32[3072]{0:T(1024)} %param.23) | copy-start | bytes 36868
Sparse Core Ops, SparseCore 0:
  44.3 45.5 all-gather.1
  147.3 65.0 reduce-scatter.1

commit v2 on v1

--- a/solution.py
+++ b/solution.py
@@ -64,8 +64,9 @@
         out_ref[k] = 2.0 * x_ref[k] - eye
 
 
-def turning(oft_skew, tenant):
+def turning(oft_skew, tenant, shares=1, share=0):
     _, count, size, _ = oft_skew.shape
+    count = count // shares
     per = next(p for p in (4, 3, 2, 1) if count % p == 0)
     return pl.pallas_call(
         functools.partial(inverse_kernel, per),
@@ -73,7 +74,7 @@
         grid_spec=pltpu.PrefetchScalarGridSpec(
             num_scalar_prefetch=1,
             grid=(count // per,),
-            in_specs=[pl.BlockSpec((1, per, size, size), lambda i, t: (t[0], i, 0, 0))],
+            in_specs=[pl.BlockSpec((1, per, size, size), lambda i, t: (t[0], t[1] + i, 0, 0))],
             out_specs=pl.BlockSpec((per, size, size), lambda i, t: (i, 0, 0)),
             scratch_shapes=[
                 pltpu.VMEM((per, size, size), BF16),
@@ -83,7 +84,7 @@
         ),
         compiler_params=pltpu.CompilerParams(vmem_limit_bytes=32 * 2**20),
         cost_estimate=pl.CostEstimate(flops=count * 50 * 2 * size**3, bytes_accessed=count * 8 * size**2, transcendentals=0),
-    )(tenant.reshape(1), oft_skew)
+    )(jnp.stack([tenant, jnp.int32(share * (count // per))]), oft_skew)
 
 
 def lay_kernel(ways, w_ref, out_ref):
@@ -135,7 +136,7 @@
     return attended.astype(BF16).reshape(-1, heads * dim)
 
 
-def per_device(
+def any_mesh(
     tokens, ln_gain, oft_skew, tenant_of_image, w_qkv, w_up, up_bias, q_gain, k_gain, w_out, w_down, down_bias
 ):
     row_count, local_width = tokens.shape
@@ -148,11 +149,7 @@
     rotation = turning(oft_skew, tenant)
     floats = tokens.astype(F32)
     sums = jnp.stack([jnp.sum(floats, 1), jnp.sum(floats * floats, 1)])
-    if ways == 2:
-        swap = functools.partial(lax.ppermute, axis_name="gy", perm=[(0, 1), (1, 0)])
-        sums = sums + swap(sums)
-    else:
-        sums = lax.psum(sums, "gy")
+    sums = lax.psum(sums, "gy")
     row_mean = sums[0][:, None] / full_width
     row_var = sums[1][:, None] / full_width - row_mean * row_mean
     normed = (floats - row_mean) * lax.rsqrt(row_var + 1e-06) * ln_gain
@@ -164,42 +161,108 @@
 
     qkv_cols, up_cols = w_first.shape[1], w_up.shape[1]
     w_attn = w_out.reshape(-1, w_out.shape[2])
-    if ways == 2:
-        half = every.shape[0] // 2
-        mine = lax.dynamic_slice_in_dim(every, gy * half, half, 0)
-        theirs = lax.dynamic_slice_in_dim(every, (1 - gy) * half, half, 0)
-        cut = up_cols // 3
-        pieces = [w_first] + [w_up[:, k * cut : (k + 1) * cut] for k in range(3)]
-        got = [swap(dot(theirs, w).astype(BF16)) for w in pieces]
-        own = [dot(mine, w) for w in pieces]
-        summed = [a + b.astype(F32) for a, b in zip(own, got)]
-        acts = [attention(summed[0], q_gain, k_gain)]
-        for k in range(3):
-            pre = summed[k + 1] + up_bias[k * cut : (k + 1) * cut]
-            acts.append(jax.nn.gelu(pre, approximate=False).astype(BF16))
-        others = [swap(a) for a in acts]
-        mixed_own = dot(acts[0], w_attn) + dot(jnp.concatenate(acts[1:], 1), w_down)
-        mixed_other = dot(others[0], w_attn) + dot(jnp.concatenate(others[1:], 1), w_down)
-        mixed_own, mixed_other = mixed_own.astype(BF16), mixed_other.astype(BF16)
-        first = gy == 0
-        mixed = jnp.concatenate(
-            [jnp.where(first, mixed_own, mixed_other), jnp.where(first, mixed_other, mixed_own)], 0
-        )
-    else:
-        part = jnp.concatenate([dot(every, w_first), dot(every, w_up)], 1)
-        summed = lax.psum_scatter(part.astype(BF16), "gy", scatter_dimension=0, tiled=True).astype(F32)
-        acts = jnp.concatenate(
-            [
-                attention(summed[:, :qkv_cols], q_gain, k_gain),
-                jax.nn.gelu(summed[:, qkv_cols:] + up_bias, approximate=False).astype(BF16),
-            ],
-            1,
-        )
-        acts = lax.all_gather(acts, "gy", axis=0, tiled=True)
-        heads_cols = w_attn.shape[0]
-        mixed = (dot(acts[:, :heads_cols], w_attn) + dot(acts[:, heads_cols:], w_down)).astype(BF16)
+    part = jnp.concatenate([dot(every, w_first), dot(every, w_up)], 1)
+    summed = lax.psum_scatter(part.astype(BF16), "gy", scatter_dimension=0, tiled=True).astype(F32)
+    acts = jnp.concatenate(
+        [
+            attention(summed[:, :qkv_cols], q_gain, k_gain),
+            jax.nn.gelu(summed[:, qkv_cols:] + up_bias, approximate=False).astype(BF16),
+        ],
+        1,
+    )
+    acts = lax.all_gather(acts, "gy", axis=0, tiled=True)
+    heads_cols = w_attn.shape[0]
+    mixed = (dot(acts[:, :heads_cols], w_attn) + dot(acts[:, heads_cols:], w_down)).astype(BF16)
     mixed = lax.psum_scatter(mixed, "gx", scatter_dimension=0, tiled=True)
     return (floats + mixed.astype(F32) + down_bias).astype(BF16)
+
+
+def swap_gy(a):
+    return lax.ppermute(a, "gy", [(0, 1), (1, 0)])
+
+
+def swap_gx(a, bit):
+    return lax.ppermute(a, "gx", [(i, i ^ bit) for i in range(16)])
+
+
+def pair(bit_set, mine, got, axis):
+    return jnp.concatenate([jnp.where(bit_set, got, mine), jnp.where(bit_set, mine, got)], axis)
+
+
+def small_mesh(
+    tokens, ln_gain, oft_skew, tenant_of_image, w_qkv, w_up, up_bias, q_gain, k_gain, w_out, w_down, down_bias
+):
+    rows, width = tokens.shape
+    gx, gy = lax.axis_index("gx"), lax.axis_index("gy")
+    core, y_bit, z_high = gx % 2, (gx // 2) % 2, gx // 8
+    dot = functools.partial(jnp.dot, preferred_element_type=F32)
+    half, quarter = width // 2, width // 4
+
+    tenant = lax.dynamic_index_in_dim(tenant_of_image, gx * rows // PATCHES, 0, keepdims=False)
+    rotation = turning(oft_skew, tenant, 4, core * 2 + y_bit)
+    floats = tokens.astype(F32)
+    sums = jnp.stack([jnp.sum(floats, 1), jnp.sum(floats * floats, 1)])
+    sums = sums + swap_gy(sums)
+    row_mean = sums[0][:, None] / (2 * width)
+    row_var = sums[1][:, None] / (2 * width) - row_mean * row_mean
+    normed = (floats - row_mean) * lax.rsqrt(row_var + 1e-06) * ln_gain
+
+    def part(a, index, size):
+        return lax.dynamic_slice_in_dim(a, index * size, size, 1)
+
+    block = pair(core == 1, part(normed, core, half), swap_gx(part(normed, 1 - core, half), 1), 0)
+    block = pair(y_bit == 1, part(block, y_bit, quarter), swap_gx(part(block, 1 - y_bit, quarter), 2), 0)
+    count, size = rotation.shape[:2]
+    turned = jnp.einsum("pnb,nbc->pnc", block.reshape(4 * rows, count, size), rotation, precision=HIGH)
+    turned = turned.reshape(4 * rows, quarter).astype(BF16)
+    w_first = lay_qkv(w_qkv)
+
+    cut = quarter // 2
+    strips = []
+    for s in range(2):
+        a = turned[None, None, :, s * cut : (s + 1) * cut]
+        a = jnp.concatenate([a, swap_gx(a, 8)], 0)
+        a = jnp.concatenate([a, swap_gx(a, 4)], 1)
+        a = a.reshape(2, 8 * rows, 1, cut)
+        got = swap_gx(a, 2)
+        a = pair(y_bit == 1, a, got, 2)
+        got = swap_gx(a, 1)
+        strips.append(pair(core == 1, a, got, 2))
+    every = jnp.stack(strips, 3).reshape(2, 8 * rows, width)
+    mine = lax.dynamic_index_in_dim(every, z_high ^ gy, 0, keepdims=False)
+    theirs = lax.dynamic_index_in_dim(every, z_high ^ gy ^ 1, 0, keepdims=False)
+
+    w_attn = w_out.reshape(-1, w_out.shape[2])
+    third = w_up.shape[1] // 3
+    pieces = [w_first] + [w_up[:, k * third : (k + 1) * third] for k in range(3)]
+    got = [swap_gy(dot(theirs, w).astype(BF16)) for w in pieces]
+    own = [dot(mine, w) for w in pieces]
+    summed = [a + b.astype(F32) for a, b in zip(own, got)]
+    acts = [attention(summed[0], q_gain, k_gain)]
+    for k in range(3):
+        pre = summed[k + 1] + up_bias[k * third : (k + 1) * third]
+        acts.append(jax.nn.gelu(pre, approximate=False).astype(BF16))
+    others = [swap_gy(a) for a in acts]
+
+    def reduced(attended, hidden, cols):
+        a = dot(attended, w_attn[:, cols]) + dot(hidden, w_down[:, cols])
+        a = a.reshape(2, 2, 2, rows, -1)
+        sent = lax.dynamic_index_in_dim(a, 1 - core, 2, keepdims=False).astype(BF16)
+        a = lax.dynamic_index_in_dim(a, core, 2, keepdims=False) + swap_gx(sent, 1).astype(F32)
+        sent = lax.dynamic_index_in_dim(a, 1 - y_bit, 1, keepdims=False).astype(BF16)
+        a = lax.dynamic_index_in_dim(a, y_bit, 1, keepdims=False) + swap_gx(sent, 2).astype(F32)
+        return a[0] + swap_gx(a[1].astype(BF16), 4).astype(F32)
+
+    spans = [slice(0, half), slice(half, width)]
+    hidden = jnp.concatenate(acts[1:], 1)
+    first = [reduced(acts[0], hidden, cols) for cols in spans]
+    hidden = jnp.concatenate(others[1:], 1)
+    second = [reduced(others[0], hidden, cols) for cols in spans]
+    here = z_high == gy
+    mixed = []
+    for a, b in zip(first, second):
+        mixed.append(jnp.where(here, a, b) + swap_gx(jnp.where(here, b, a).astype(BF16), 8).astype(F32))
+    return (floats + jnp.concatenate(mixed, 1) + down_bias).astype(BF16)
 
 
 def solution(mesh):
@@ -217,4 +280,6 @@
         P("gx", "gy"),
         P("gy"),
     )
+    small = dict(mesh.shape) == {"gx": 16, "gy": 2}
+    per_device = small_mesh if small else any_mesh
     return jax.shard_map(per_device, mesh=mesh, in_specs=in_specs, out_specs=P("gx", "gy"), check_vma=False)

time: 221 us -> 170 us (0.77)
  waiting for transfers between devices: 109 us -> 53.6 us
  starting transfers between devices: 11.6 us -> 43 us
  Pallas kernels: 37.5 us -> 18.1 us
  between operations: 13.7 us -> 0.86 us
  other arithmetic: 5.91 us -> 8.98 us
    reduce_scatter x1 -> x0, waiting for transfers between devices: 65.2 us -> none  [per_device(): mixed = lax.psum_scatter(mixed, 'gx', scatter_dimension=0, tiled=True)]
    ppermute x9 -> x33, waiting for transfers between devices: 6.3 us -> 53.6 us  [the longest x24 37.3 us: swap_gx(): return lax.ppermute(a, 'gx', [(i, i ^ bit) for i in range(16)])]
    all_gather x1 -> x0, waiting for transfers between devices: 37.4 us -> none  [per_device(): every = lax.all_gather(turned, 'gx', axis=0, tiled=True)]
    ppermute x9 -> x33, starting transfers between devices: 11.6 us -> 43 us  [the longest x24 31.7 us: swap_gx(): return lax.ppermute(a, 'gx', [(i, i ^ bit) for i in range(16)])]
    pallas_call x1, Pallas kernels: 29.3 us -> 9.89 us  [turning(): pl.pallas_call(functools.partial(inverse_kernel, per), out_shape=jax.Shap...]
    another operation x0 -> x1, local copies, waits for them, and re-layouts: none -> 2.98 us  [small_mesh(): every = jnp.stack(strips, 3).reshape(2, 8 * rows, width)]
    dot_general x13 -> x17, matrix products: 38.2 us -> 37.7 us  [the longest x8 15.6 us: reduced(): a = dot(attended, w_attn[:, cols]) + dot(hidden, w_down[:, cols])]
  transfers between devices with their start and end apart: 11 -> 33, of which waited for: 5 -> 13; matrix products, arithmetic and copies ran while one was open for 17% -> 21% of each run, Pallas kernels for 17% -> 11%
where the time goes in v2:
time: 170 us
  waiting for transfers between devices  53.6 us (32%)
  starting transfers between devices  43 us (25%)
  matrix products  38.6 us (23%)
  Pallas kernels  18.1 us (11%)
  other arithmetic  8.98 us (5%)
  local copies, waits for them, and re-layouts  6.28 us (4%)
    ppermute x24, waiting for transfers between devices, swap_gx(): return lax.ppermute(a, 'gx', [(i, i ^ bit) for i in range(16)])  37.3 us
    ppermute x24, starting transfers between devices, swap_gx(): return lax.ppermute(a, 'gx', [(i, i ^ bit) for i in range(16)])  31.7 us
    ppermute x9, waiting for transfers between devices, swap_gy(): return lax.ppermute(a, 'gy', [(0, 1), (1, 0)])  16.3 us
    dot_general x8, matrix products, reduced(): a = dot(attended, w_attn[:, cols]) + dot(hidden, w_down[:, cols])  15.6 us
    ppermute x9, starting transfers between devices, swap_gy(): return lax.ppermute(a, 'gy', [(0, 1), (1, 0)])  11.4 us
    dot_general x4, matrix products, small_mesh(): got = [swap_gy(dot(theirs, w).astype(BF16)) for w in pieces]  11.2 us
    pallas_call x1, Pallas kernels, turning(): pl.pallas_call(functools.partial(inverse_kernel, per), out_shape=jax.Shap...  9.89 us
    dot_general x4, matrix products, small_mesh(): own = [dot(mine, w) for w in pieces]  9.39 us
  transfers between devices with their start and end apart: 33, of which 13 were waited for; matrix products, arithmetic and copies ran while one was open for 21% of the time, Pallas kernels for 11%

profile of v2, /device:TPU:0, one launch (start us, length us, event | category | flops | bytes accessed | tf_op | source)
XLA Modules:
  0.0 169.5 jit_solution(10114295739181654033)
XLA Ops:
  0.0 1.1 convert_reduce_fusion
  1.1 3.0 %collective-permute-start = (f32[2,32]{1,0:T(2,128)S(1)}, f32[2,32]{1,0:T(2,128)S(1)}, u32[]{:S(2)}, u32[]{:S(2)}) collective-permute-start(f32[2,32]{1,0:T(2,128)S(1)} %pad_maximum_fusion.11), channel_id=1, source_target_pairs={{0,1},{1,0},{2,3},{3,2},{4,5},{5,4},{6,7},{7,6},{8,9},{9,8},{10,11... | collective-permute-start | bytes 776 | tf_op jit(solution)/shard_map/ppermute | solution.py:181
  4.1 1.5 collective-permute-done
  5.7 1.1 fusion.95
  6.9 1.3 dynamic_slice.73
  8.2 0.7 pad_add_fusion.tenant_ref
  9.0 2.1 %collective-permute-start.2 = (f32[64,768]{1,0:T(8,128)S(1)}, f32[64,768]{1,0:T(8,128)S(1)}, u32[]{:S(2)}, u32[]{:S(2)}) collective-permute-start(f32[64,768]{1,0:T(8,128)S(1)} %fusion.113), channel_id=1, source_target_pairs={{0,4},{2,6},{4,0},{6,2},{8,12},{10,14},{12,8},{14,10},{16,20},{18,... | collective-permute-start | bytes 589832 | tf_op jit(solution)/shard_map/ppermute | solution.py:185
  11.1 9.9 %shard_map.118 = f32[3,256,256]{2,1,0:T(8,128)S(1)} custom-call(s32[2]{0:T(128)S(1)} %pad_add_fusion.tenant_ref, f32[8,12,256,256]{3,2,1,0:T(8,128)} %skew_ref.1), custom_call_target="tpu_custom_call" | custom-call | flops 5033164800 | bytes 1572864 | tf_op jit(solution)/shard_map/pallas_call | solution.py:71
  21.3 1.4 convolution_convert_fusion
  22.8 2.7 %collective-permute-start.7 = (bf16[1,1,128,384]{3,2,1,0:T(8,128)(2,1)S(1)}, bf16[1,1,128,384]{3,2,1,0:T(8,128)(2,1)S(1)}, u32[]{:S(2)}, u32[]{:S(2)}) collective-permute-start(bf16[1,1,128,384]{3,2,1,0:T(8,128)(2,1)S(1)} %bitcast.227), channel_id=1, source_target_pairs={{0,16},{2,18},{4,20},{6,22},{8,24},{10,26},{12,28},{14,30},{16,0},... | collective-permute-start | bytes 294920 | tf_op jit(solution)/shard_map/ppermute | solution.py:185
  25.5 5.3 %collective-permute-done.7 = bf16[1,1,128,384]{3,2,1,0:T(8,128)(2,1)S(1)} collective-permute-done((bf16[1,1,128,384]{3,2,1,0:T(8,128)(2,1)S(1)}, bf16[1,1,128,384]{3,2,1,0:T(8,128)(2,1)S(1)}, u32[]{:S(2)}, u32[]{:S(2)}) %collective-permute-start.7) | collective-permute-done | bytes 98336 | tf_op jit(solution)/shard_map/ppermute | solution.py:185
  30.8 0.7 collective-permute-start.8
  31.7 3.4 %collective-permute-start.3 = (bf16[1,1,128,384]{3,2,1,0:T(8,128)(2,1)S(1)}, bf16[1,1,128,384]{3,2,1,0:T(8,128)(2,1)S(1)}, u32[]{:S(2)}, u32[]{:S(2)}) collective-permute-start(bf16[1,1,128,384]{3,2,1,0:T(8,128)(2,1)S(1)} %bitcast.224), channel_id=1, source_target_pairs={{0,16},{2,18},{4,20},{6,22},{8,24},{10,26},{12,28},{14,30},{16,0},... | collective-permute-start | bytes 294920 | tf_op jit(solution)/shard_map/ppermute | solution.py:185
  35.1 4.0 %collective-permute-done.8 = bf16[2,1,128,384]{3,2,1,0:T(8,128)(2,1)S(1)} collective-permute-done((bf16[2,1,128,384]{3,2,1,0:T(8,128)(2,1)S(1)}, bf16[2,1,128,384]{3,2,1,0:T(8,128)(2,1)S(1)}, u32[]{:S(2)}, u32[]{:S(2)}) %collective-permute-start.8) | collective-permute-done | bytes 196640 | tf_op jit(solution)/shard_map/ppermute | solution.py:185
  39.2 0.8 collective-permute-start.9
  40.0 2.2 %collective-permute-start.4 = (bf16[2,1,128,384]{3,2,1,0:T(8,128)(2,1)S(1)}, bf16[2,1,128,384]{3,2,1,0:T(8,128)(2,1)S(1)}, u32[]{:S(2)}, u32[]{:S(2)}) collective-permute-start(bf16[2,1,128,384]{3,2,1,0:T(8,128)(2,1)S(1)} %pad_maximum_fusion.9), channel_id=1, source_target_pairs={{0,8},{2,10},{4,12},{6,14},{8,0},{10,2},{12,4},{14,6},{16,24},{18,... | collective-permute-start | bytes 589832 | tf_op jit(solution)/shard_map/ppermute | solution.py:185
  42.2 4.6 %collective-permute-done.4 = bf16[2,1,128,384]{3,2,1,0:T(8,128)(2,1)S(1)} collective-permute-done((bf16[2,1,128,384]{3,2,1,0:T(8,128)(2,1)S(1)}, bf16[2,1,128,384]{3,2,1,0:T(8,128)(2,1)S(1)}, u32[]{:S(2)}, u32[]{:S(2)}) %collective-permute-start.4) | collective-permute-done | bytes 196640 | tf_op jit(solution)/shard_map/ppermute | solution.py:185
  46.8 0.6 collective-permute-start.5
  47.4 0.8 collective-permute-done.9
  48.4 1.0 pad_maximum_fusion.2
  49.4 7.4 %collective-permute-done.5 = bf16[2,256,1,384]{3,1,0,2:T(8,128)(2,1)S(1)} collective-permute-done((bf16[2,256,1,384]{3,1,0,2:T(8,128)(2,1)S(1)}, bf16[2,256,1,384]{3,1,0,2:T(8,128)(2,1)S(1)}, u32[]{:S(2)}, u32[]{:S(2)}) %collective-permute-start.5) | collective-permute-done | bytes 393248 | tf_op jit(solution)/shard_map/ppermute | solution.py:185
  57.0 1.0 pad_maximum_fusion.1
  58.0 8.2 %shard_map.119 = bf16[3072,768]{1,0:T(8,128)(2,1)} custom-call(bf16[18432,128]{1,0:T(8,128)(2,1)} %bitcast.210), custom_call_target="tpu_custom_call" | custom-call | flops 1811939328 | bytes 9437184 | tf_op jit(solution)/shard_map/pallas_call | solution.py:108
  67.3 3.0 %copy.69 = bf16[2,256,4,2,384]{1,4,3,2,0:T(8,128)(2,1)} copy(bf16[2,256,4,2,384]{4,1,0,2,3:T(8,128)(2,1)S(1)} %pad_maximum_fusion) | data formatting | bytes 6291456 | tf_op jit(solution)/shard_map/stack | solution.py:231
  70.3 3.5 %fusion.46 = bf16[256,512]{1,0:T(8,128)(2,1)S(1)} fusion(bf16[3072,1536]{1,0:T(8,128)(2,1)} %param.17, bf16[2,256,3072]{1,2,0:T(8,128)(2,1)} %bitcast.213, s32[]{:T(128)S(6)} %select_n.180), kind=kOutput, calls=%fused_computation.44 | convolution fusion | flops 805437440 | bytes 4980740 | tf_op jit(solution)/shard_map/dot_general | solution.py:238
  73.8 3.0 %fusion.41 = bf16[256,512]{1,0:T(8,128)(2,1)S(1)} fusion(bf16[3072,1536]{1,0:T(8,128)(2,1)} %param.17, bf16[2,256,3072]{1,2,0:T(8,128)(2,1)S(1)} %bitcast.214, s32[]{:T(128)S(6)} %select_n.180), kind=kOutput, calls=%fused_computation.43 | convolution fusion | flops 805437440 | bytes 4980740 | tf_op jit(solution)/shard_map/dot_general | solution.py:238
  76.9 3.2 %fusion.36 = bf16[256,512]{1,0:T(8,128)(2,1)S(1)} fusion(bf16[3072,1536]{1,0:T(8,128)(2,1)} %param.17, bf16[2,256,3072]{1,2,0:T(8,128)(2,1)S(1)} %bitcast.215, s32[]{:T(128)S(6)} %select_n.180), kind=kOutput, calls=%fused_computation.42 | convolution fusion | flops 805437440 | bytes 4980740 | tf_op jit(solution)/shard_map/dot_general | solution.py:238
  80.2 1.6 collective-permute-start.14
  82.3 1.5 collective-permute-start.12
  83.8 1.4 fusion.32
  85.2 0.6 collective-permute-start.11
  85.8 14.8 %collective-permute-done.12 = bf16[256,512]{1,0:T(8,128)(2,1)S(1)} collective-permute-done((bf16[256,512]{1,0:T(8,128)(2,1)S(1)}, bf16[256,512]{1,0:T(8,128)(2,1)S(1)}, u32[]{:S(2)}, u32[]{:S(2)}) %collective-permute-start.12) | collective-permute-done | bytes 262176 | tf_op jit(solution)/shard_map/ppermute | solution.py:181
  100.6 2.1 %fusion.65 = bf16[256,512]{1,0:T(8,128)(2,1)S(1)} fusion(bf16[256,512]{1,0:T(8,128)(2,1)S(1)} %collective-permute-done.12, f32[512]{0:T(512)S(1)} %get-tuple-element.25, bf16[3072,1536]{1,0:T(8,128)(2,1)S(1)} %bitcast.239, bf16[2,256,3072]{1,2,0:T(8,128)(2,1)S(1)} %bitcast.217, s32[]{:T(128)S(6)} %select_n.179), kind=kOutput, calls=%fused_computation.84 | convolution fusion | flops 814219264 | bytes 5244932 | tf_op jit(solution)/shard_map/dot_general | solution.py:239
  102.7 1.6 collective-permute-start.19
  104.3 2.8 %fusion.68 = bf16[256,512]{1,0:T(8,128)(2,1)} fusion(bf16[256,512]{1,0:T(8,128)(2,1)S(1)} %collective-permute-done.13, f32[512]{0:T(512)S(1)} %get-tuple-element.27, bf16[3072,1536]{1,0:T(8,128)(2,1)S(1)} %bitcast.239, bf16[2,256,3072]{1,2,0:T(8,128)(2,1)S(1)} %bitcast.218, s32[]{:T(128)S(6)} %select_n.179), kind=kOutput, calls=%fused_computation.87 | convolution fusion | flops 814219264 | bytes 5244932 | tf_op jit(solution)/shard_map/dot_general | solution.py:239
  107.6 2.8 %fusion.71 = bf16[256,512]{1,0:T(8,128)(2,1)} fusion(bf16[256,512]{1,0:T(8,128)(2,1)S(1)} %collective-permute-done.14, f32[512]{0:T(512)S(1)} %get-tuple-element.26, bf16[3072,1536]{1,0:T(8,128)(2,1)S(1)} %bitcast.239, bf16[2,256,3072]{1,2,0:T(8,128)(2,1)S(1)} %bitcast.219, s32[]{:T(128)S(6)} %select_n.179), kind=kOutput, calls=%fused_computation.90 | convolution fusion | flops 814219264 | bytes 5244932 | tf_op jit(solution)/shard_map/dot_general | solution.py:239
  110.4 1.5 collective-permute-start.21
  112.0 3.7 %fusion.3 = f32[256,1536]{1,0:T(8,128)} fusion(bf16[1536,3072]{1,0:T(8,128)(2,1)S(1)} %bitcast.241, bf16[256,512]{1,0:T(8,128)(2,1)} %fusion.71, bf16[256,512]{1,0:T(8,128)(2,1)} %fusion.68, bf16[256,512]{1,0:T(8,128)(2,1)S(1)} %fusion.65), kind=kOutput, calls=%fused_computation.3 | convolution fusion | flops 1210318848 | bytes 7077888 | tf_op jit(solution)/shard_map/dot_general | solution.py:248
  115.6 3.6 %fusion.7 = f32[256,1536]{1,0:T(8,128)} fusion(bf16[1536,3072]{1,0:T(8,128)(2,1)S(1)} %bitcast.241, bf16[256,512]{1,0:T(8,128)(2,1)} %fusion.71, bf16[256,512]{1,0:T(8,128)(2,1)} %fusion.68, bf16[256,512]{1,0:T(8,128)(2,1)S(1)} %fusion.65), kind=kOutput, calls=%fused_computation.7 | convolution fusion | flops 1210318848 | bytes 7077888 | tf_op jit(solution)/shard_map/dot_general | solution.py:248
  119.3 1.7 convert_add_fusion
  121.4 0.6 slice_reduce_fusion.1
  122.6 0.7 convolution_multiply_fusion
  123.9 0.6 collective-permute-start.18
  124.7 1.9 %convolution_add_fusion.1 = f32[256,1536]{1,0:T(8,128)S(1)} fusion(f32[256,1536]{1,0:T(8,128)} %fusion.3, bf16[256,256]{0,1:T(8,128)(2,1)S(1)} %bitcast.232, bf16[256,3072]{1,0:T(8,128)(2,1)S(1)} %bitcast.198), kind=kOutput, calls=%fused_computation.11 | convolution fusion | flops 201719808 | bytes 4063232 | tf_op jit(solution)/shard_map/dot_general | solution.py:248
  128.0 3.8 %fusion.1 = f32[256,1536]{1,0:T(8,128)S(1)} fusion(bf16[256,1536]{1,0:T(8,128)(2,1)S(1)} %constant_dynamic-update-slice_fusion, bf16[1536,3072]{1,0:T(8,128)(2,1)} %param.22), kind=kOutput, calls=%fused_computation.1 | convolution fusion | flops 1207959552 | bytes 7077888 | tf_op jit(solution)/shard_map/dot_general | solution.py:248
  131.9 1.4 fusion.5
  134.3 0.6 collective-permute-start.22
  135.0 1.1 collective-permute-start.27
  136.2 1.0 collective-permute-start.16
  137.4 1.1 collective-permute-start.30
  138.6 1.0 collective-permute-start.23
  139.6 3.1 %collective-permute-done.27 = bf16[2,32,1536]{2,1,0:T(8,128)(2,1)S(1)} collective-permute-done((bf16[2,32,1536]{2,1,0:T(8,128)(2,1)S(1)}, bf16[2,32,1536]{2,1,0:T(8,128)(2,1)S(1)}, u32[]{:S(2)}, u32[]{:S(2)}) %collective-permute-start.27) | collective-permute-done | bytes 196640 | tf_op jit(solution)/shard_map/ppermute | solution.py:185
  142.8 1.5 collective-permute-start.28
  144.3 2.7 %collective-permute-done.16 = bf16[2,32,1536]{2,1,0:T(8,128)(2,1)S(1)} collective-permute-done((bf16[2,32,1536]{2,1,0:T(8,128)(2,1)S(1)}, bf16[2,32,1536]{2,1,0:T(8,128)(2,1)S(1)}, u32[]{:S(2)}, u32[]{:S(2)}) %collective-permute-start.16) | collective-permute-done | bytes 196640 | tf_op jit(solution)/shard_map/ppermute | solution.py:185
  147.1 1.5 collective-permute-start.17
  148.6 2.7 %collective-permute-done.30 = bf16[2,32,1536]{2,1,0:T(8,128)(2,1)S(1)} collective-permute-done((bf16[2,32,1536]{2,1,0:T(8,128)(2,1)S(1)}, bf16[2,32,1536]{2,1,0:T(8,128)(2,1)S(1)}, u32[]{:S(2)}, u32[]{:S(2)}) %collective-permute-start.30) | collective-permute-done | bytes 196640 | tf_op jit(solution)/shard_map/ppermute | solution.py:185
  151.3 1.5 collective-permute-start.31
  152.8 1.7 %collective-permute-done.23 = bf16[2,32,1536]{2,1,0:T(8,128)(2,1)S(1)} collective-permute-done((bf16[2,32,1536]{2,1,0:T(8,128)(2,1)S(1)}, bf16[2,32,1536]{2,1,0:T(8,128)(2,1)S(1)}, u32[]{:S(2)}, u32[]{:S(2)}) %collective-permute-start.23) | collective-permute-done | bytes 196640 | tf_op jit(solution)/shard_map/ppermute | solution.py:185
  154.6 1.5 collective-permute-start.24
  156.1 4.4 %collective-permute-start.32 = (bf16[32,1536]{1,0:T(8,128)(2,1)S(1)}, bf16[32,1536]{1,0:T(8,128)(2,1)S(1)}, u32[]{:S(2)}, u32[]{:S(2)}) collective-permute-start(bf16[32,1536]{1,0:T(8,128)(2,1)S(1)} %select_convert_fusion), channel_id=1, source_target_pairs={{0,16},{2,18},{4,20},{6,22},{8,24},{10,26},{12,28},{14,30},{16,0},... | collective-permute-start | bytes 294920 | tf_op jit(solution)/shard_map/ppermute | solution.py:185
  160.6 3.1 %collective-permute-start.25 = (bf16[32,1536]{1,0:T(8,128)(2,1)S(1)}, bf16[32,1536]{1,0:T(8,128)(2,1)S(1)}, u32[]{:S(2)}, u32[]{:S(2)}) collective-permute-start(bf16[32,1536]{1,0:T(8,128)(2,1)S(1)} %select_convert_fusion.1), channel_id=1, source_target_pairs={{0,16},{2,18},{4,20},{6,22},{8,24},{10,26},{12,28},{14,30},{16,0},... | collective-permute-start | bytes 294920 | tf_op jit(solution)/shard_map/ppermute | solution.py:185
  163.7 2.5 %collective-permute-done.32 = bf16[32,1536]{1,0:T(8,128)(2,1)S(1)} collective-permute-done((bf16[32,1536]{1,0:T(8,128)(2,1)S(1)}, bf16[32,1536]{1,0:T(8,128)(2,1)S(1)}, u32[]{:S(2)}, u32[]{:S(2)}) %collective-permute-start.32) | collective-permute-done | bytes 98336 | tf_op jit(solution)/shard_map/ppermute | solution.py:185
  166.3 2.4 %collective-permute-done.25 = bf16[32,1536]{1,0:T(8,128)(2,1)S(1)} collective-permute-done((bf16[32,1536]{1,0:T(8,128)(2,1)S(1)}, bf16[32,1536]{1,0:T(8,128)(2,1)S(1)}, u32[]{:S(2)}, u32[]{:S(2)}) %collective-permute-start.25) | collective-permute-done | bytes 98336 | tf_op jit(solution)/shard_map/ppermute | solution.py:185
  168.8 0.7 fusion.97
  (135 shorter events, 8.1 us)
Async XLA Ops:
  1.1 4.6 %collective-permute-start = (f32[2,32]{1,0:T(2,128)S(1)}, f32[2,32]{1,0:T(2,128)S(1)}, u32[]{:S(2)}, u32[]{:S(2)}) collective-permute-start(f32[2,32]{1,0:T(2,128)S(1)} %pad_maximum_fusion.11), channel_id=1, source_target_pairs={{0,1},{1,0},{2,3},{3,2},{4,5},{5,4},{6,7},{7,6},{8,9},{9,8},{10,11... | collective-permute-start | bytes 776 | tf_op jit(solution)/shard_map/ppermute | solution.py:181
  6.8 2.2 %collective-permute-start.1 = (f32[32,1536]{1,0:T(8,128)S(1)}, f32[32,1536]{1,0:T(8,128)S(1)}, u32[]{:S(2)}, u32[]{:S(2)}) collective-permute-start(f32[32,1536]{1,0:T(8,128)S(1)} %constant_dynamic-slice_fusion), channel_id=1, source_target_pairs={{0,2},{2,0},{4,6},{6,4},{8,10},{10,8},{12,14},{14,12},{16,18},{18,... | collective-permute-start | bytes 589832 | tf_op jit(solution)/shard_map/ppermute | solution.py:185
  9.0 12.0 %collective-permute-start.2 = (f32[64,768]{1,0:T(8,128)S(1)}, f32[64,768]{1,0:T(8,128)S(1)}, u32[]{:S(2)}, u32[]{:S(2)}) collective-permute-start(f32[64,768]{1,0:T(8,128)S(1)} %fusion.113), channel_id=1, source_target_pairs={{0,4},{2,6},{4,0},{6,2},{8,12},{10,14},{12,8},{14,10},{16,20},{18,... | collective-permute-start | bytes 589832 | tf_op jit(solution)/shard_map/ppermute | solution.py:185
  22.8 7.9 %collective-permute-start.7 = (bf16[1,1,128,384]{3,2,1,0:T(8,128)(2,1)S(1)}, bf16[1,1,128,384]{3,2,1,0:T(8,128)(2,1)S(1)}, u32[]{:S(2)}, u32[]{:S(2)}) collective-permute-start(bf16[1,1,128,384]{3,2,1,0:T(8,128)(2,1)S(1)} %bitcast.227), channel_id=1, source_target_pairs={{0,16},{2,18},{4,20},{6,22},{8,24},{10,26},{12,28},{14,30},{16,0},... | collective-permute-start | bytes 294920 | tf_op jit(solution)/shard_map/ppermute | solution.py:185
  30.8 8.3 %collective-permute-start.8 = (bf16[2,1,128,384]{3,2,1,0:T(8,128)(2,1)S(1)}, bf16[2,1,128,384]{3,2,1,0:T(8,128)(2,1)S(1)}, u32[]{:S(2)}, u32[]{:S(2)}) collective-permute-start(bf16[2,1,128,384]{3,2,1,0:T(8,128)(2,1)S(1)} %pad_maximum_fusion.10), channel_id=1, source_target_pairs={{0,8},{2,10},{4,12},{6,14},{8,0},{10,2},{12,4},{14,6},{16,24},{18,... | collective-permute-start | bytes 589832 | tf_op jit(solution)/shard_map/ppermute | solution.py:185
  31.7 8.3 %collective-permute-start.3 = (bf16[1,1,128,384]{3,2,1,0:T(8,128)(2,1)S(1)}, bf16[1,1,128,384]{3,2,1,0:T(8,128)(2,1)S(1)}, u32[]{:S(2)}, u32[]{:S(2)}) collective-permute-start(bf16[1,1,128,384]{3,2,1,0:T(8,128)(2,1)S(1)} %bitcast.224), channel_id=1, source_target_pairs={{0,16},{2,18},{4,20},{6,22},{8,24},{10,26},{12,28},{14,30},{16,0},... | collective-permute-start | bytes 294920 | tf_op jit(solution)/shard_map/ppermute | solution.py:185
  39.2 9.1 %collective-permute-start.9 = (bf16[2,256,1,384]{3,1,0,2:T(8,128)(2,1)S(1)}, bf16[2,256,1,384]{3,1,0,2:T(8,128)(2,1)S(1)}, u32[]{:S(2)}, u32[]{:S(2)}) collective-permute-start(bf16[2,256,1,384]{3,1,0,2:T(8,128)(2,1)S(1)} %bitcast.221), channel_id=1, source_target_pairs={{0,4},{2,6},{4,0},{6,2},{8,12},{10,14},{12,8},{14,10},{16,20},{18,... | collective-permute-start | bytes 1179656 | tf_op jit(solution)/shard_map/ppermute | solution.py:185
  40.0 6.8 %collective-permute-start.4 = (bf16[2,1,128,384]{3,2,1,0:T(8,128)(2,1)S(1)}, bf16[2,1,128,384]{3,2,1,0:T(8,128)(2,1)S(1)}, u32[]{:S(2)}, u32[]{:S(2)}) collective-permute-start(bf16[2,1,128,384]{3,2,1,0:T(8,128)(2,1)S(1)} %pad_maximum_fusion.9), channel_id=1, source_target_pairs={{0,8},{2,10},{4,12},{6,14},{8,0},{10,2},{12,4},{14,6},{16,24},{18,... | collective-permute-start | bytes 589832 | tf_op jit(solution)/shard_map/ppermute | solution.py:185
  46.8 10.0 %collective-permute-start.5 = (bf16[2,256,1,384]{3,1,0,2:T(8,128)(2,1)S(1)}, bf16[2,256,1,384]{3,1,0,2:T(8,128)(2,1)S(1)}, u32[]{:S(2)}, u32[]{:S(2)}) collective-permute-start(bf16[2,256,1,384]{3,1,0,2:T(8,128)(2,1)S(1)} %bitcast.222), channel_id=1, source_target_pairs={{0,4},{2,6},{4,0},{6,2},{8,12},{10,14},{12,8},{14,10},{16,20},{18,... | collective-permute-start | bytes 1179656 | tf_op jit(solution)/shard_map/ppermute | solution.py:185
  49.4 16.8 %collective-permute-start.10 = (bf16[2,256,2,384]{3,1,0,2:T(8,128)(2,1)}, bf16[2,256,2,384]{3,1,0,2:T(8,128)(2,1)S(1)}, u32[]{:S(2)}, u32[]{:S(2)}) collective-permute-start(bf16[2,256,2,384]{3,1,0,2:T(8,128)(2,1)} %pad_maximum_fusion.2), channel_id=1, source_target_pairs={{0,2},{2,0},{4,6},{6,4},{8,10},{10,8},{12,14},{14,12},{16,18},{18,... | collective-permute-start | bytes 2359304 | tf_op jit(solution)/shard_map/ppermute | solution.py:185
  57.9 8.2 %collective-permute-start.6 = (bf16[2,256,2,384]{3,1,0,2:T(8,128)(2,1)}, bf16[2,256,2,384]{3,1,0,2:T(8,128)(2,1)S(1)}, u32[]{:S(2)}, u32[]{:S(2)}) collective-permute-start(bf16[2,256,2,384]{3,1,0,2:T(8,128)(2,1)} %pad_maximum_fusion.1), channel_id=1, source_target_pairs={{0,2},{2,0},{4,6},{6,4},{8,10},{10,8},{12,14},{14,12},{16,18},{18,... | collective-permute-start | bytes 2359304 | tf_op jit(solution)/shard_map/ppermute | solution.py:185
  58.0 8.2 %copy-start.5 = (f32[1536]{0:T(1024)S(1)}, f32[1536]{0:T(1024)}, u32[]{:S(2)}) copy-start(f32[1536]{0:T(1024)} %param.18) | copy-start | bytes 18436
  70.3 3.5 %copy-start.1 = (bf16[2,256,4,2,384]{1,4,3,2,0:T(8,128)(2,1)S(1)}, bf16[2,256,4,2,384]{1,4,3,2,0:T(8,128)(2,1)}, u32[]{:S(2)}) copy-start(bf16[2,256,4,2,384]{1,4,3,2,0:T(8,128)(2,1)} %copy.69) | copy-start | bytes 9437188
  73.8 10.0 %slice-start = ((s8[4718592]{0:T(1024)(128)(4,1)}), s8[4194304]{0:T(1024)(128)(4,1)S(1)}, s32[]{:S(2)}) async-start(s8[4718592]{0:T(1024)(128)(4,1)} %bitcast.211), calls=%async_computation | async-start | bytes 8388608
  73.8 26.8 %slice-start.2 = ((s8[9437184]{0:T(1024)(128)(4,1)}), s8[4194304]{0:T(1024)(128)(4,1)S(1)}, s32[]{:S(2)}) async-start(s8[9437184]{0:T(1024)(128)(4,1)} %bitcast.238), calls=%async_computation.2 | async-start | bytes 8388608
  76.9 6.9 %slice-start.1 = ((s8[4718592]{0:T(1024)(128)(4,1)}), s8[524288]{0:T(1024)(128)(4,1)S(1)}, s32[]{:S(2)}) async-start(s8[4718592]{0:T(1024)(128)(4,1)} %bitcast.211), calls=%async_computation.1 | async-start | bytes 1048576
  76.9 23.7 %slice-start.3 = ((s8[9437184]{0:T(1024)(128)(4,1)}), s8[4194304]{0:T(1024)(128)(4,1)S(1)}, s32[]{:S(2)}) async-start(s8[9437184]{0:T(1024)(128)(4,1)} %bitcast.238), calls=%async_computation.3 | async-start | bytes 8388608
  80.1 20.4 %slice-start.4 = ((s8[9437184]{0:T(1024)(128)(4,1)}), s8[1048576]{0:T(1024)(128)(4,1)S(1)}, s32[]{:S(2)}) async-start(s8[9437184]{0:T(1024)(128)(4,1)} %bitcast.238), calls=%async_computation.4 | async-start | bytes 2097152
  80.2 27.4 %collective-permute-start.14 = (bf16[256,512]{1,0:T(8,128)(2,1)S(1)}, bf16[256,512]{1,0:T(8,128)(2,1)S(1)}, u32[]{:S(2)}, u32[]{:S(2)}) collective-permute-start(bf16[256,512]{1,0:T(8,128)(2,1)S(1)} %fusion.46), channel_id=1, source_target_pairs={{0,1},{1,0},{2,3},{3,2},{4,5},{5,4},{6,7},{7,6},{8,9},{9,8},{10,11... | collective-permute-start | bytes 786440 | tf_op jit(solution)/shard_map/ppermute | solution.py:181
  81.7 22.5 %collective-permute-start.13 = (bf16[256,512]{1,0:T(8,128)(2,1)S(1)}, bf16[256,512]{1,0:T(8,128)(2,1)S(1)}, u32[]{:S(2)}, u32[]{:S(2)}) collective-permute-start(bf16[256,512]{1,0:T(8,128)(2,1)S(1)} %fusion.41), channel_id=1, source_target_pairs={{0,1},{1,0},{2,3},{3,2},{4,5},{5,4},{6,7},{7,6},{8,9},{9,8},{10,11... | collective-permute-start | bytes 786440 | tf_op jit(solution)/shard_map/ppermute | solution.py:181
  82.3 18.3 %collective-permute-start.12 = (bf16[256,512]{1,0:T(8,128)(2,1)S(1)}, bf16[256,512]{1,0:T(8,128)(2,1)S(1)}, u32[]{:S(2)}, u32[]{:S(2)}) collective-permute-start(bf16[256,512]{1,0:T(8,128)(2,1)S(1)} %fusion.36), channel_id=1, source_target_pairs={{0,1},{1,0},{2,3},{3,2},{4,5},{5,4},{6,7},{7,6},{8,9},{9,8},{10,11... | collective-permute-start | bytes 786440 | tf_op jit(solution)/shard_map/ppermute | solution.py:181
  85.2 34.0 %collective-permute-start.11 = (bf16[256,768]{1,0:T(8,128)(2,1)S(1)}, bf16[256,768]{1,0:T(8,128)(2,1)S(1)}, u32[]{:S(2)}, u32[]{:S(2)}) collective-permute-start(bf16[256,768]{1,0:T(8,128)(2,1)S(1)} %fusion.32), channel_id=1, source_target_pairs={{0,1},{1,0},{2,3},{3,2},{4,5},{5,4},{6,7},{7,6},{8,9},{9,8},{10,11... | collective-permute-start | bytes 1179656 | tf_op jit(solution)/shard_map/ppermute | solution.py:181
  102.7 24.6 %collective-permute-start.19 = (bf16[256,512]{1,0:T(8,128)(2,1)S(1)}, bf16[256,512]{1,0:T(8,128)(2,1)S(1)}, u32[]{:S(2)}, u32[]{:S(2)}) collective-permute-start(bf16[256,512]{1,0:T(8,128)(2,1)S(1)} %fusion.65), channel_id=1, source_target_pairs={{0,1},{1,0},{2,3},{3,2},{4,5},{5,4},{6,7},{7,6},{8,9},{9,8},{10,11... | collective-permute-start | bytes 786440 | tf_op jit(solution)/shard_map/ppermute | solution.py:181
  104.3 7.7 %slice-start.5 = ((s8[9437184]{0:T(1024)(128)(4,1)}), s8[4194304]{0:T(1024)(128)(4,1)S(1)}, s32[]{:S(2)}) async-start(s8[9437184]{0:T(1024)(128)(4,1)} %bitcast.240), calls=%async_computation.5 | async-start | bytes 8388608
  104.3 7.7 %slice-start.6 = ((s8[9437184]{0:T(1024)(128)(4,1)}), s8[4194304]{0:T(1024)(128)(4,1)S(1)}, s32[]{:S(2)}) async-start(s8[9437184]{0:T(1024)(128)(4,1)} %bitcast.240), calls=%async_computation.6 | async-start | bytes 8388608
  107.1 20.8 %collective-permute-start.20 = (bf16[256,512]{1,0:T(8,128)(2,1)}, bf16[256,512]{1,0:T(8,128)(2,1)S(1)}, u32[]{:S(2)}, u32[]{:S(2)}) collective-permute-start(bf16[256,512]{1,0:T(8,128)(2,1)} %fusion.68), channel_id=1, source_target_pairs={{0,1},{1,0},{2,3},{3,2},{4,5},{5,4},{6,7},{7,6},{8,9},{9,8},{10,11... | collective-permute-start | bytes 786440 | tf_op jit(solution)/shard_map/ppermute | solution.py:181
  107.6 4.3 %slice-start.7 = ((s8[9437184]{0:T(1024)(128)(4,1)}), s8[1048576]{0:T(1024)(128)(4,1)S(1)}, s32[]{:S(2)}) async-start(s8[9437184]{0:T(1024)(128)(4,1)} %bitcast.240), calls=%async_computation.7 | async-start | bytes 2097152
  110.4 17.5 %collective-permute-start.21 = (bf16[256,512]{1,0:T(8,128)(2,1)}, bf16[256,512]{1,0:T(8,128)(2,1)S(1)}, u32[]{:S(2)}, u32[]{:S(2)}) collective-permute-start(bf16[256,512]{1,0:T(8,128)(2,1)} %fusion.71), channel_id=1, source_target_pairs={{0,1},{1,0},{2,3},{3,2},{4,5},{5,4},{6,7},{7,6},{8,9},{9,8},{10,11... | collective-permute-start | bytes 786440 | tf_op jit(solution)/shard_map/ppermute | solution.py:181
  121.3 1.3 copy-start.6
  121.4 1.3 copy-start.7
  123.3 1.4 copy-start
  123.9 9.4 %collective-permute-start.18 = (bf16[256,256]{0,1:T(8,128)(2,1)S(1)}, bf16[256,256]{0,1:T(8,128)(2,1)S(1)}, u32[]{:S(2)}, u32[]{:S(2)}) collective-permute-start(bf16[256,256]{0,1:T(8,128)(2,1)S(1)} %bitcast.231), channel_id=1, source_target_pairs={{0,1},{1,0},{2,3},{3,2},{4,5},{5,4},{6,7},{7,6},{8,9},{9,8},{10,11... | collective-permute-start | bytes 393224 | tf_op jit(solution)/shard_map/ppermute | solution.py:181
  124.7 2.1 %copy-start.3 = (f32[256,1536]{1,0:T(8,128)S(1)}, f32[256,1536]{1,0:T(8,128)}, u32[]{:S(2)}) copy-start(f32[256,1536]{1,0:T(8,128)} %fusion.7) | copy-start | bytes 4718596
  124.7 7.1 %slice-start.8 = ((s8[9437184]{0:T(1024)(128)(4,1)}), s8[4194304]{0:T(1024)(128)(4,1)S(1)}, s32[]{:S(2)}) async-start(s8[9437184]{0:T(1024)(128)(4,1)} %bitcast.242), calls=%async_computation.8 | async-start | bytes 8388608
  126.8 5.1 %slice-start.9 = ((s8[9437184]{0:T(1024)(128)(4,1)}), s8[4194304]{0:T(1024)(128)(4,1)S(1)}, s32[]{:S(2)}) async-start(s8[9437184]{0:T(1024)(128)(4,1)} %bitcast.242), calls=%async_computation.9 | async-start | bytes 8388608
  126.8 8.1 %collective-permute-start.26 = (bf16[2,2,32,1536]{3,2,1,0:T(8,128)(2,1)S(1)}, bf16[2,2,32,1536]{3,2,1,0:T(8,128)(2,1)S(1)}, u32[]{:S(2)}, u32[]{:S(2)}) collective-permute-start(bf16[2,2,32,1536]{3,2,1,0:T(8,128)(2,1)S(1)} %fusion.100), channel_id=1, source_target_pairs={{0,2},{2,0},{4,6},{6,4},{8,10},{10,8},{12,14},{14,12},{16,18},{18,... | collective-permute-start | bytes 1179656 | tf_op jit(solution)/shard_map/ppermute | solution.py:185
  127.3 8.8 %collective-permute-start.15 = (bf16[2,2,32,1536]{3,2,1,0:T(8,128)(2,1)S(1)}, bf16[2,2,32,1536]{3,2,1,0:T(8,128)(2,1)S(1)}, u32[]{:S(2)}, u32[]{:S(2)}) collective-permute-start(bf16[2,2,32,1536]{3,2,1,0:T(8,128)(2,1)S(1)} %fusion.98), channel_id=1, source_target_pairs={{0,2},{2,0},{4,6},{6,4},{8,10},{10,8},{12,14},{14,12},{16,18},{18,... | collective-permute-start | bytes 1179656 | tf_op jit(solution)/shard_map/ppermute | solution.py:185
  128.0 3.9 %slice-start.10 = ((s8[9437184]{0:T(1024)(128)(4,1)}), s8[1048576]{0:T(1024)(128)(4,1)S(1)}, s32[]{:S(2)}) async-start(s8[9437184]{0:T(1024)(128)(4,1)} %bitcast.242), calls=%async_computation.10 | async-start | bytes 2097152
  133.7 3.5 %collective-permute-start.29 = (bf16[2,2,32,1536]{3,2,1,0:T(8,128)(2,1)S(1)}, bf16[2,2,32,1536]{3,2,1,0:T(8,128)(2,1)S(1)}, u32[]{:S(2)}, u32[]{:S(2)}) collective-permute-start(bf16[2,2,32,1536]{3,2,1,0:T(8,128)(2,1)S(1)} %fusion.101), channel_id=1, source_target_pairs={{0,2},{2,0},{4,6},{6,4},{8,10},{10,8},{12,14},{14,12},{16,18},{18,... | collective-permute-start | bytes 1179656 | tf_op jit(solution)/shard_map/ppermute | solution.py:185
  134.3 4.2 %collective-permute-start.22 = (bf16[2,2,32,1536]{3,2,1,0:T(8,128)(2,1)S(1)}, bf16[2,2,32,1536]{3,2,1,0:T(8,128)(2,1)S(1)}, u32[]{:S(2)}, u32[]{:S(2)}) collective-permute-start(bf16[2,2,32,1536]{3,2,1,0:T(8,128)(2,1)S(1)} %fusion.99), channel_id=1, source_target_pairs={{0,2},{2,0},{4,6},{6,4},{8,10},{10,8},{12,14},{14,12},{16,18},{18,... | collective-permute-start | bytes 1179656 | tf_op jit(solution)/shard_map/ppermute | solution.py:185
  135.0 7.8 %collective-permute-start.27 = (bf16[2,32,1536]{2,1,0:T(8,128)(2,1)S(1)}, bf16[2,32,1536]{2,1,0:T(8,128)(2,1)S(1)}, u32[]{:S(2)}, u32[]{:S(2)}) collective-permute-start(bf16[2,32,1536]{2,1,0:T(8,128)(2,1)S(1)} %fusion.110), channel_id=1, source_target_pairs={{0,4},{2,6},{4,0},{6,2},{8,12},{10,14},{12,8},{14,10},{16,20},{18,... | collective-permute-start | bytes 589832 | tf_op jit(solution)/shard_map/ppermute | solution.py:185
  136.2 10.8 %collective-permute-start.16 = (bf16[2,32,1536]{2,1,0:T(8,128)(2,1)S(1)}, bf16[2,32,1536]{2,1,0:T(8,128)(2,1)S(1)}, u32[]{:S(2)}, u32[]{:S(2)}) collective-permute-start(bf16[2,32,1536]{2,1,0:T(8,128)(2,1)S(1)} %fusion.108), channel_id=1, source_target_pairs={{0,4},{2,6},{4,0},{6,2},{8,12},{10,14},{12,8},{14,10},{16,20},{18,... | collective-permute-start | bytes 589832 | tf_op jit(solution)/shard_map/ppermute | solution.py:185
  137.4 13.8 %collective-permute-start.30 = (bf16[2,32,1536]{2,1,0:T(8,128)(2,1)S(1)}, bf16[2,32,1536]{2,1,0:T(8,128)(2,1)S(1)}, u32[]{:S(2)}, u32[]{:S(2)}) collective-permute-start(bf16[2,32,1536]{2,1,0:T(8,128)(2,1)S(1)} %fusion.111), channel_id=1, source_target_pairs={{0,4},{2,6},{4,0},{6,2},{8,12},{10,14},{12,8},{14,10},{16,20},{18,... | collective-permute-start | bytes 589832 | tf_op jit(solution)/shard_map/ppermute | solution.py:185
  138.6 15.9 %collective-permute-start.23 = (bf16[2,32,1536]{2,1,0:T(8,128)(2,1)S(1)}, bf16[2,32,1536]{2,1,0:T(8,128)(2,1)S(1)}, u32[]{:S(2)}, u32[]{:S(2)}) collective-permute-start(bf16[2,32,1536]{2,1,0:T(8,128)(2,1)S(1)} %fusion.109), channel_id=1, source_target_pairs={{0,4},{2,6},{4,0},{6,2},{8,12},{10,14},{12,8},{14,10},{16,20},{18,... | collective-permute-start | bytes 589832 | tf_op jit(solution)/shard_map/ppermute | solution.py:185
  142.8 13.2 %collective-permute-start.28 = (bf16[32,1536]{1,0:T(8,128)(2,1)S(1)}, bf16[32,1536]{1,0:T(8,128)(2,1)S(1)}, u32[]{:S(2)}, u32[]{:S(2)}) collective-permute-start(bf16[32,1536]{1,0:T(8,128)(2,1)S(1)} %fusion.130), channel_id=1, source_target_pairs={{0,8},{2,10},{4,12},{6,14},{8,0},{10,2},{12,4},{14,6},{16,24},{18,... | collective-permute-start | bytes 294920 | tf_op jit(solution)/shard_map/ppermute | solution.py:185
  147.1 13.5 %collective-permute-start.17 = (bf16[32,1536]{1,0:T(8,128)(2,1)S(1)}, bf16[32,1536]{1,0:T(8,128)(2,1)S(1)}, u32[]{:S(2)}, u32[]{:S(2)}) collective-permute-start(bf16[32,1536]{1,0:T(8,128)(2,1)S(1)} %fusion.128), channel_id=1, source_target_pairs={{0,8},{2,10},{4,12},{6,14},{8,0},{10,2},{12,4},{14,6},{16,24},{18,... | collective-permute-start | bytes 294920 | tf_op jit(solution)/shard_map/ppermute | solution.py:185
  151.3 4.8 %collective-permute-start.31 = (bf16[32,1536]{1,0:T(8,128)(2,1)S(1)}, bf16[32,1536]{1,0:T(8,128)(2,1)S(1)}, u32[]{:S(2)}, u32[]{:S(2)}) collective-permute-start(bf16[32,1536]{1,0:T(8,128)(2,1)S(1)} %fusion.131), channel_id=1, source_target_pairs={{0,8},{2,10},{4,12},{6,14},{8,0},{10,2},{12,4},{14,6},{16,24},{18,... | collective-permute-start | bytes 294920 | tf_op jit(solution)/shard_map/ppermute | solution.py:185
  154.6 14.2 %copy-start.2 = (bf16[32,3072]{1,0:T(8,128)(2,1)S(1)}, bf16[32,3072]{1,0:T(8,128)(2,1)}, u32[]{:S(2)}) copy-start(bf16[32,3072]{1,0:T(8,128)(2,1)} %param.12) | copy-start | bytes 589828
  154.6 14.2 %copy-start.4 = (f32[3072]{0:T(1024)S(1)}, f32[3072]{0:T(1024)}, u32[]{:S(2)}) copy-start(f32[3072]{0:T(1024)} %param.23) | copy-start | bytes 36868
  154.6 6.0 %collective-permute-start.24 = (bf16[32,1536]{1,0:T(8,128)(2,1)S(1)}, bf16[32,1536]{1,0:T(8,128)(2,1)S(1)}, u32[]{:S(2)}, u32[]{:S(2)}) collective-permute-start(bf16[32,1536]{1,0:T(8,128)(2,1)S(1)} %fusion.129), channel_id=1, source_target_pairs={{0,8},{2,10},{4,12},{6,14},{8,0},{10,2},{12,4},{14,6},{16,24},{18,... | collective-permute-start | bytes 294920 | tf_op jit(solution)/shard_map/ppermute | solution.py:185
  156.1 10.1 %collective-permute-start.32 = (bf16[32,1536]{1,0:T(8,128)(2,1)S(1)}, bf16[32,1536]{1,0:T(8,128)(2,1)S(1)}, u32[]{:S(2)}, u32[]{:S(2)}) collective-permute-start(bf16[32,1536]{1,0:T(8,128)(2,1)S(1)} %select_convert_fusion), channel_id=1, source_target_pairs={{0,16},{2,18},{4,20},{6,22},{8,24},{10,26},{12,28},{14,30},{16,0},... | collective-permute-start | bytes 294920 | tf_op jit(solution)/shard_map/ppermute | solution.py:185
  160.6 8.1 %collective-permute-start.25 = (bf16[32,1536]{1,0:T(8,128)(2,1)S(1)}, bf16[32,1536]{1,0:T(8,128)(2,1)S(1)}, u32[]{:S(2)}, u32[]{:S(2)}) collective-permute-start(bf16[32,1536]{1,0:T(8,128)(2,1)S(1)} %select_convert_fusion.1), channel_id=1, source_target_pairs={{0,16},{2,18},{4,20},{6,22},{8,24},{10,26},{12,28},{14,30},{16,0},... | collective-permute-start | bytes 294920 | tf_op jit(solution)/shard_map/ppermute | solution.py:185

commit v3 on v2

--- a/solution.py
+++ b/solution.py
@@ -225,6 +225,8 @@
         a = jnp.concatenate([a, swap_gx(a, 4)], 1)
         a = a.reshape(2, 8 * rows, 1, cut)
         got = swap_gx(a, 2)
+        if s == 0:
+            got, w_first = lax.optimization_barrier((got, w_first))
         a = pair(y_bit == 1, a, got, 2)
         got = swap_gx(a, 1)
         strips.append(pair(core == 1, a, got, 2))
@@ -236,11 +238,11 @@
     third = w_up.shape[1] // 3
     pieces = [w_first] + [w_up[:, k * third : (k + 1) * third] for k in range(3)]
     got = [swap_gy(dot(theirs, w).astype(BF16)) for w in pieces]
-    own = [dot(mine, w) for w in pieces]
-    summed = [a + b.astype(F32) for a, b in zip(own, got)]
-    acts = [attention(summed[0], q_gain, k_gain)]
+    own = [lax.optimization_barrier(dot(mine, w)) for w in pieces]
+    acts = [attention(own[0] + got[0].astype(F32), q_gain, k_gain)]
+    got[2], acts[0] = lax.optimization_barrier((got[2], acts[0]))
     for k in range(3):
-        pre = summed[k + 1] + up_bias[k * third : (k + 1) * third]
+        pre = own[k + 1] + got[k + 1].astype(F32) + up_bias[k * third : (k + 1) * third]
         acts.append(jax.nn.gelu(pre, approximate=False).astype(BF16))
     others = [swap_gy(a) for a in acts]
 

time: 170 us -> 172 us (1.012)
  waiting for transfers between devices: 53.6 us -> 61.7 us
  matrix products: 38.6 us -> 31.5 us
  other arithmetic: 8.98 us -> 14.3 us
  starting transfers between devices: 43 us -> 38.9 us
    ppermute x9, waiting for transfers between devices: 16.3 us -> 21.9 us  [swap_gy(): return lax.ppermute(a, 'gy', [(0, 1), (1, 0)])]
    convert_element_type x0 -> x3, other arithmetic: none -> 5.24 us  [small_mesh(): acts.append(jax.nn.gelu(pre, approximate=False).astype(BF16))]
    ppermute x24, starting transfers between devices: 31.7 us -> 26.6 us  [swap_gx(): return lax.ppermute(a, 'gx', [(i, i ^ bit) for i in range(16)])]
    dot_general x8, matrix products: 15.6 us -> 12.1 us  [reduced(): a = dot(attended, w_attn[:, cols]) + dot(hidden, w_down[:, cols])]
    dot_general x4, matrix products: 9.39 us -> 6.45 us  [small_mesh(): own = [lax.optimization_barrier(dot(mine, w)) for w in pieces]]
    ppermute x24, waiting for transfers between devices: 37.3 us -> 39.8 us  [swap_gx(): return lax.ppermute(a, 'gx', [(i, i ^ bit) for i in range(16)])]
  transfers between devices with their start and end apart: 33 -> 33, of which waited for: 13 -> 14; matrix products, arithmetic and copies ran while one was open for 21% -> 16% of each run, Pallas kernels for 11% -> 11%
where the time goes in v3:
time: 172 us; the launch traced here: 171 us
  waiting for transfers between devices  61.7 us (36%)
  starting transfers between devices  38.9 us (23%)
  matrix products  31.5 us (18%)
  Pallas kernels  18.1 us (11%)
  other arithmetic  14.3 us (8%)
  local copies, waits for them, and re-layouts  5.97 us (3%)
    ppermute x24, waiting for transfers between devices, swap_gx(): return lax.ppermute(a, 'gx', [(i, i ^ bit) for i in range(16)])  39.8 us
    ppermute x24, starting transfers between devices, swap_gx(): return lax.ppermute(a, 'gx', [(i, i ^ bit) for i in range(16)])  26.6 us
    ppermute x9, waiting for transfers between devices, swap_gy(): return lax.ppermute(a, 'gy', [(0, 1), (1, 0)])  21.9 us
    ppermute x9, starting transfers between devices, swap_gy(): return lax.ppermute(a, 'gy', [(0, 1), (1, 0)])  12.3 us
    dot_general x8, matrix products, reduced(): a = dot(attended, w_attn[:, cols]) + dot(hidden, w_down[:, cols])  12.1 us
    dot_general x4, matrix products, small_mesh(): got = [swap_gy(dot(theirs, w).astype(BF16)) for w in pieces]  10.4 us
    pallas_call x1, Pallas kernels, turning(): pl.pallas_call(functools.partial(inverse_kernel, per), out_shape=jax.Shap...  9.91 us
    pallas_call x1, Pallas kernels, lay_qkv(): pl.pallas_call(functools.partial(lay_kernel, ways), out_shape=jax.ShapeDt...  8.18 us
  transfers between devices with their start and end apart: 33, of which 14 were waited for; matrix products, arithmetic and copies ran while one was open for 16% of the time, Pallas kernels for 11%

profile of v3, /device:TPU:0, one launch (start us, length us, event | category | flops | bytes accessed | tf_op | source)
XLA Modules:
  0.0 171.4 jit_solution(8153350326651899135)
XLA Ops:
  0.0 1.1 convert_reduce_fusion
  1.1 3.0 %collective-permute-start = (f32[2,32]{1,0:T(2,128)S(1)}, f32[2,32]{1,0:T(2,128)S(1)}, u32[]{:S(2)}, u32[]{:S(2)}) collective-permute-start(f32[2,32]{1,0:T(2,128)S(1)} %pad_maximum_fusion.11), channel_id=1, source_target_pairs={{0,1},{1,0},{2,3},{3,2},{4,5},{5,4},{6,7},{7,6},{8,9},{9,8},{10,11... | collective-permute-start | bytes 776 | tf_op jit(solution)/shard_map/ppermute | solution.py:181
  4.1 1.5 collective-permute-done
  5.7 1.1 fusion.95
  6.9 1.3 dynamic_slice.73
  8.2 0.7 pad_add_fusion.tenant_ref
  9.0 2.1 %collective-permute-start.2 = (f32[64,768]{1,0:T(8,128)S(1)}, f32[64,768]{1,0:T(8,128)S(1)}, u32[]{:S(2)}, u32[]{:S(2)}) collective-permute-start(f32[64,768]{1,0:T(8,128)S(1)} %fusion.113), channel_id=1, source_target_pairs={{0,4},{2,6},{4,0},{6,2},{8,12},{10,14},{12,8},{14,10},{16,20},{18,... | collective-permute-start | bytes 589832 | tf_op jit(solution)/shard_map/ppermute | solution.py:185
  11.1 9.9 %shard_map.118 = f32[3,256,256]{2,1,0:T(8,128)S(1)} custom-call(s32[2]{0:T(128)S(1)} %pad_add_fusion.tenant_ref, f32[8,12,256,256]{3,2,1,0:T(8,128)} %skew_ref.1), custom_call_target="tpu_custom_call" | custom-call | flops 5033164800 | bytes 1572864 | tf_op jit(solution)/shard_map/pallas_call | solution.py:71
  21.3 1.4 convolution_convert_fusion
  22.8 2.7 %collective-permute-start.3 = (bf16[1,1,128,384]{3,2,1,0:T(8,128)(2,1)S(1)}, bf16[1,1,128,384]{3,2,1,0:T(8,128)(2,1)S(1)}, u32[]{:S(2)}, u32[]{:S(2)}) collective-permute-start(bf16[1,1,128,384]{3,2,1,0:T(8,128)(2,1)S(1)} %bitcast.219), channel_id=1, source_target_pairs={{0,16},{2,18},{4,20},{6,22},{8,24},{10,26},{12,28},{14,30},{16,0},... | collective-permute-start | bytes 294920 | tf_op jit(solution)/shard_map/ppermute | solution.py:185
  25.5 5.2 %collective-permute-done.3 = bf16[1,1,128,384]{3,2,1,0:T(8,128)(2,1)S(1)} collective-permute-done((bf16[1,1,128,384]{3,2,1,0:T(8,128)(2,1)S(1)}, bf16[1,1,128,384]{3,2,1,0:T(8,128)(2,1)S(1)}, u32[]{:S(2)}, u32[]{:S(2)}) %collective-permute-start.3) | collective-permute-done | bytes 98336 | tf_op jit(solution)/shard_map/ppermute | solution.py:185
  30.7 0.8 collective-permute-start.4
  31.6 3.4 %collective-permute-start.7 = (bf16[1,1,128,384]{3,2,1,0:T(8,128)(2,1)S(1)}, bf16[1,1,128,384]{3,2,1,0:T(8,128)(2,1)S(1)}, u32[]{:S(2)}, u32[]{:S(2)}) collective-permute-start(bf16[1,1,128,384]{3,2,1,0:T(8,128)(2,1)S(1)} %bitcast.216), channel_id=1, source_target_pairs={{0,16},{2,18},{4,20},{6,22},{8,24},{10,26},{12,28},{14,30},{16,0},... | collective-permute-start | bytes 294920 | tf_op jit(solution)/shard_map/ppermute | solution.py:185
  35.0 3.9 %collective-permute-done.4 = bf16[2,1,128,384]{3,2,1,0:T(8,128)(2,1)S(1)} collective-permute-done((bf16[2,1,128,384]{3,2,1,0:T(8,128)(2,1)S(1)}, bf16[2,1,128,384]{3,2,1,0:T(8,128)(2,1)S(1)}, u32[]{:S(2)}, u32[]{:S(2)}) %collective-permute-start.4) | collective-permute-done | bytes 196640 | tf_op jit(solution)/shard_map/ppermute | solution.py:185
  39.0 1.0 collective-permute-start.5
  40.1 2.1 %collective-permute-start.8 = (bf16[2,1,128,384]{3,2,1,0:T(8,128)(2,1)S(1)}, bf16[2,1,128,384]{3,2,1,0:T(8,128)(2,1)S(1)}, u32[]{:S(2)}, u32[]{:S(2)}) collective-permute-start(bf16[2,1,128,384]{3,2,1,0:T(8,128)(2,1)S(1)} %pad_maximum_fusion.10), channel_id=1, source_target_pairs={{0,8},{2,10},{4,12},{6,14},{8,0},{10,2},{12,4},{14,6},{16,24},{18,... | collective-permute-start | bytes 589832 | tf_op jit(solution)/shard_map/ppermute | solution.py:185
  42.2 8.2 %shard_map.119 = bf16[3072,768]{1,0:T(8,128)(2,1)} custom-call(bf16[18432,128]{1,0:T(8,128)(2,1)} %bitcast.202), custom_call_target="tpu_custom_call" | custom-call | flops 1811939328 | bytes 9437184 | tf_op jit(solution)/shard_map/pallas_call | solution.py:108
  50.4 0.6 collective-permute-start.9
  51.1 1.0 pad_maximum_fusion.1
  52.1 8.6 %collective-permute-done.9 = bf16[2,256,1,384]{3,1,0,2:T(8,128)(2,1)S(1)} collective-permute-done((bf16[2,256,1,384]{3,1,0,2:T(8,128)(2,1)S(1)}, bf16[2,256,1,384]{3,1,0,2:T(8,128)(2,1)S(1)}, u32[]{:S(2)}, u32[]{:S(2)}) %collective-permute-start.9) | collective-permute-done | bytes 393248 | tf_op jit(solution)/shard_map/ppermute | solution.py:185
  60.8 1.0 pad_maximum_fusion.2
  61.9 2.5 %collective-permute-done.10 = bf16[2,256,2,384]{3,1,0,2:T(8,128)(2,1)S(1)} collective-permute-done((bf16[2,256,2,384]{3,1,0,2:T(8,128)(2,1)}, bf16[2,256,2,384]{3,1,0,2:T(8,128)(2,1)S(1)}, u32[]{:S(2)}, u32[]{:S(2)}) %collective-permute-start.10) | collective-permute-done | bytes 786464 | tf_op jit(solution)/shard_map/ppermute | solution.py:185
  65.4 3.0 %copy.69 = bf16[2,256,4,2,384]{1,4,3,2,0:T(8,128)(2,1)} copy(bf16[2,256,4,2,384]{4,1,0,2,3:T(8,128)(2,1)S(1)} %pad_maximum_fusion) | data formatting | bytes 6291456 | tf_op jit(solution)/shard_map/stack | solution.py:233
  68.4 3.5 %fusion.41 = bf16[256,512]{1,0:T(8,128)(2,1)S(1)} fusion(bf16[3072,1536]{1,0:T(8,128)(2,1)} %param.17, bf16[2,256,3072]{1,2,0:T(8,128)(2,1)} %bitcast.205, s32[]{:T(128)S(6)} %select_n.179), kind=kOutput, calls=%fused_computation.43 | convolution fusion | flops 805437440 | bytes 4980740 | tf_op jit(solution)/shard_map/dot_general | solution.py:240
  71.9 3.0 %fusion.15 = f32[256,512]{1,0:T(8,128)S(1)} fusion(bf16[3072,1536]{1,0:T(8,128)(2,1)} %param.17, bf16[2,256,3072]{1,2,0:T(8,128)(2,1)S(1)} %bitcast.206, s32[]{:T(128)S(6)} %select_n.180), kind=kOutput, calls=%fused_computation.20 | convolution fusion | flops 805306368 | bytes 5242884 | tf_op jit(solution)/shard_map/dot_general | solution.py:241
  75.0 4.1 %fusion.32 = bf16[256,768]{1,0:T(8,128)(2,1)S(1)} fusion(bf16[3072,768]{1,0:T(8,128)(2,1)} %shard_map.119, bf16[2,256,3072]{1,2,0:T(8,128)(2,1)S(1)} %bitcast.207, s32[]{:T(128)S(6)} %select_n.179), kind=kOutput, calls=%fused_computation.39 | convolution fusion | flops 1208156160 | bytes 6684676 | tf_op jit(solution)/shard_map/dot_general | solution.py:240
  79.2 1.4 fusion.24
  80.7 1.7 %fusion.36 = bf16[256,512]{1,0:T(8,128)(2,1)} fusion(bf16[3072,1536]{1,0:T(8,128)(2,1)S(1)} %bitcast.231, bf16[2,256,3072]{1,2,0:T(8,128)(2,1)S(1)} %bitcast.209, s32[]{:T(128)S(6)} %select_n.179), kind=kOutput, calls=%fused_computation.42 | convolution fusion | flops 805437440 | bytes 4980740 | tf_op jit(solution)/shard_map/dot_general | solution.py:240
  82.4 1.0 fusion.17
  83.4 1.0 fusion.46
  84.4 1.6 collective-permute-start.13
  86.5 1.5 collective-permute-start.11
  88.5 1.0 fusion.11
  89.5 4.1 %collective-permute-done.13 = bf16[256,512]{1,0:T(8,128)(2,1)S(1)} collective-permute-done((bf16[256,512]{1,0:T(8,128)(2,1)S(1)}, bf16[256,512]{1,0:T(8,128)(2,1)S(1)}, u32[]{:S(2)}, u32[]{:S(2)}) %collective-permute-start.13) | collective-permute-done | bytes 262176 | tf_op jit(solution)/shard_map/ppermute | solution.py:181
  93.6 1.9 %fusion.65 = bf16[256,512]{1,0:T(8,128)(2,1)} fusion(f32[256,512]{1,0:T(8,128)S(1)} %fusion.15, bf16[256,512]{1,0:T(8,128)(2,1)S(1)} %collective-permute-done.13, f32[512]{0:T(512)S(1)} %get-tuple-element.33), kind=kLoop, calls=%fused_computation.84 | loop fusion | flops 8912896 | bytes 1050624 | tf_op jit(solution)/shard_map/convert_element_type | solution.py:246
  95.5 1.5 collective-permute-start.19
  97.0 16.3 %collective-permute-done.14 = bf16[256,512]{1,0:T(8,128)(2,1)S(1)} collective-permute-done((bf16[256,512]{1,0:T(8,128)(2,1)S(1)}, bf16[256,512]{1,0:T(8,128)(2,1)S(1)}, u32[]{:S(2)}, u32[]{:S(2)}) %collective-permute-start.14) | collective-permute-done | bytes 262176 | tf_op jit(solution)/shard_map/ppermute | solution.py:181
  113.3 1.2 fusion.71
  114.5 1.6 collective-permute-start.21
  116.6 0.6 slice_reduce_fusion.1
  117.7 0.9 convolution_multiply_fusion
  119.3 2.1 %fusion.68 = bf16[256,512]{1,0:T(8,128)(2,1)S(1)} fusion(f32[256,512]{1,0:T(8,128)S(1)} %fusion.17, bf16[256,512]{1,0:T(8,128)(2,1)} %collective-permute-done.11, f32[512]{0:T(512)S(1)} %get-tuple-element.35), kind=kLoop, calls=%fused_computation.87 | loop fusion | flops 8912896 | bytes 1050624 | tf_op jit(solution)/shard_map/convert_element_type | solution.py:246
  121.4 0.6 collective-permute-start.20
  122.0 3.8 %fusion.7 = f32[256,1536]{1,0:T(8,128)S(1)} fusion(bf16[1536,3072]{1,0:T(8,128)(2,1)} %param.22, bf16[256,512]{1,0:T(8,128)(2,1)S(1)} %fusion.71, bf16[256,512]{1,0:T(8,128)(2,1)S(1)} %fusion.68, bf16[256,512]{1,0:T(8,128)(2,1)} %fusion.65), kind=kOutput, calls=%fused_computation.7 | convolution fusion | flops 1210318848 | bytes 7077888 | tf_op jit(solution)/shard_map/dot_general | solution.py:250
  125.9 3.9 %fusion.3 = f32[256,1536]{1,0:T(8,128)S(1)} fusion(bf16[1536,3072]{1,0:T(8,128)(2,1)} %param.22, bf16[256,512]{1,0:T(8,128)(2,1)S(1)} %fusion.71, bf16[256,512]{1,0:T(8,128)(2,1)S(1)} %fusion.68, bf16[256,512]{1,0:T(8,128)(2,1)} %fusion.65), kind=kOutput, calls=%fused_computation.3 | convolution fusion | flops 1210318848 | bytes 7077888 | tf_op jit(solution)/shard_map/dot_general | solution.py:250
  129.8 1.6 collective-permute-start.18
  132.4 0.6 collective-permute-start.26
  133.1 1.4 fusion.5
  134.5 1.4 fusion.1
  137.6 0.6 collective-permute-start.16
  138.3 1.5 collective-permute-start.27
  139.8 5.5 %collective-permute-done.16 = bf16[2,32,1536]{2,1,0:T(8,128)(2,1)S(1)} collective-permute-done((bf16[2,32,1536]{2,1,0:T(8,128)(2,1)S(1)}, bf16[2,32,1536]{2,1,0:T(8,128)(2,1)S(1)}, u32[]{:S(2)}, u32[]{:S(2)}) %collective-permute-start.16) | collective-permute-done | bytes 196640 | tf_op jit(solution)/shard_map/ppermute | solution.py:185
  145.9 2.8 %collective-permute-done.27 = bf16[2,32,1536]{2,1,0:T(8,128)(2,1)S(1)} collective-permute-done((bf16[2,32,1536]{2,1,0:T(8,128)(2,1)S(1)}, bf16[2,32,1536]{2,1,0:T(8,128)(2,1)S(1)}, u32[]{:S(2)}, u32[]{:S(2)}) %collective-permute-start.27) | collective-permute-done | bytes 196640 | tf_op jit(solution)/shard_map/ppermute | solution.py:185
  149.3 0.6 collective-permute-start.23
  150.0 1.6 collective-permute-start.30
  151.6 5.6 %collective-permute-done.23 = bf16[2,32,1536]{2,1,0:T(8,128)(2,1)S(1)} collective-permute-done((bf16[2,32,1536]{2,1,0:T(8,128)(2,1)S(1)}, bf16[2,32,1536]{2,1,0:T(8,128)(2,1)S(1)}, u32[]{:S(2)}, u32[]{:S(2)}) %collective-permute-start.23) | collective-permute-done | bytes 196640 | tf_op jit(solution)/shard_map/ppermute | solution.py:185
  157.2 1.7 %collective-permute-start.24 = (bf16[32,1536]{1,0:T(8,128)(2,1)S(1)}, bf16[32,1536]{1,0:T(8,128)(2,1)S(1)}, u32[]{:S(2)}, u32[]{:S(2)}) collective-permute-start(bf16[32,1536]{1,0:T(8,128)(2,1)S(1)} %fusion.129), channel_id=1, source_target_pairs={{0,8},{2,10},{4,12},{6,14},{8,0},{10,2},{12,4},{14,6},{16,24},{18,... | collective-permute-start | bytes 294920 | tf_op jit(solution)/shard_map/ppermute | solution.py:185
  159.4 1.7 %collective-permute-start.31 = (bf16[32,1536]{1,0:T(8,128)(2,1)S(1)}, bf16[32,1536]{1,0:T(8,128)(2,1)S(1)}, u32[]{:S(2)}, u32[]{:S(2)}) collective-permute-start(bf16[32,1536]{1,0:T(8,128)(2,1)S(1)} %fusion.131), channel_id=1, source_target_pairs={{0,8},{2,10},{4,12},{6,14},{8,0},{10,2},{12,4},{14,6},{16,24},{18,... | collective-permute-start | bytes 294920 | tf_op jit(solution)/shard_map/ppermute | solution.py:185
  161.1 1.0 collective-permute-done.24
  162.1 2.7 %collective-permute-start.25 = (bf16[32,1536]{1,0:T(8,128)(2,1)S(1)}, bf16[32,1536]{1,0:T(8,128)(2,1)S(1)}, u32[]{:S(2)}, u32[]{:S(2)}) collective-permute-start(bf16[32,1536]{1,0:T(8,128)(2,1)S(1)} %select_convert_fusion.1), channel_id=1, source_target_pairs={{0,16},{2,18},{4,20},{6,22},{8,24},{10,26},{12,28},{14,30},{16,0},... | collective-permute-start | bytes 294920 | tf_op jit(solution)/shard_map/ppermute | solution.py:185
  164.9 1.3 collective-permute-start.32
  166.2 3.3 %collective-permute-done.25 = bf16[32,1536]{1,0:T(8,128)(2,1)S(1)} collective-permute-done((bf16[32,1536]{1,0:T(8,128)(2,1)S(1)}, bf16[32,1536]{1,0:T(8,128)(2,1)S(1)}, u32[]{:S(2)}, u32[]{:S(2)}) %collective-permute-start.25) | collective-permute-done | bytes 98336 | tf_op jit(solution)/shard_map/ppermute | solution.py:185
  169.6 1.0 collective-permute-done.32
  170.6 0.7 fusion.97
  (130 shorter events, 9.5 us)
Async XLA Ops:
  1.1 4.6 %collective-permute-start = (f32[2,32]{1,0:T(2,128)S(1)}, f32[2,32]{1,0:T(2,128)S(1)}, u32[]{:S(2)}, u32[]{:S(2)}) collective-permute-start(f32[2,32]{1,0:T(2,128)S(1)} %pad_maximum_fusion.11), channel_id=1, source_target_pairs={{0,1},{1,0},{2,3},{3,2},{4,5},{5,4},{6,7},{7,6},{8,9},{9,8},{10,11... | collective-permute-start | bytes 776 | tf_op jit(solution)/shard_map/ppermute | solution.py:181
  6.8 2.1 %collective-permute-start.1 = (f32[32,1536]{1,0:T(8,128)S(1)}, f32[32,1536]{1,0:T(8,128)S(1)}, u32[]{:S(2)}, u32[]{:S(2)}) collective-permute-start(f32[32,1536]{1,0:T(8,128)S(1)} %constant_dynamic-slice_fusion), channel_id=1, source_target_pairs={{0,2},{2,0},{4,6},{6,4},{8,10},{10,8},{12,14},{14,12},{16,18},{18,... | collective-permute-start | bytes 589832 | tf_op jit(solution)/shard_map/ppermute | solution.py:185
  9.0 12.0 %collective-permute-start.2 = (f32[64,768]{1,0:T(8,128)S(1)}, f32[64,768]{1,0:T(8,128)S(1)}, u32[]{:S(2)}, u32[]{:S(2)}) collective-permute-start(f32[64,768]{1,0:T(8,128)S(1)} %fusion.113), channel_id=1, source_target_pairs={{0,4},{2,6},{4,0},{6,2},{8,12},{10,14},{12,8},{14,10},{16,20},{18,... | collective-permute-start | bytes 589832 | tf_op jit(solution)/shard_map/ppermute | solution.py:185
  22.8 7.9 %collective-permute-start.3 = (bf16[1,1,128,384]{3,2,1,0:T(8,128)(2,1)S(1)}, bf16[1,1,128,384]{3,2,1,0:T(8,128)(2,1)S(1)}, u32[]{:S(2)}, u32[]{:S(2)}) collective-permute-start(bf16[1,1,128,384]{3,2,1,0:T(8,128)(2,1)S(1)} %bitcast.219), channel_id=1, source_target_pairs={{0,16},{2,18},{4,20},{6,22},{8,24},{10,26},{12,28},{14,30},{16,0},... | collective-permute-start | bytes 294920 | tf_op jit(solution)/shard_map/ppermute | solution.py:185
  30.7 8.2 %collective-permute-start.4 = (bf16[2,1,128,384]{3,2,1,0:T(8,128)(2,1)S(1)}, bf16[2,1,128,384]{3,2,1,0:T(8,128)(2,1)S(1)}, u32[]{:S(2)}, u32[]{:S(2)}) collective-permute-start(bf16[2,1,128,384]{3,2,1,0:T(8,128)(2,1)S(1)} %pad_maximum_fusion.9), channel_id=1, source_target_pairs={{0,8},{2,10},{4,12},{6,14},{8,0},{10,2},{12,4},{14,6},{16,24},{18,... | collective-permute-start | bytes 589832 | tf_op jit(solution)/shard_map/ppermute | solution.py:185
  31.6 8.4 %collective-permute-start.7 = (bf16[1,1,128,384]{3,2,1,0:T(8,128)(2,1)S(1)}, bf16[1,1,128,384]{3,2,1,0:T(8,128)(2,1)S(1)}, u32[]{:S(2)}, u32[]{:S(2)}) collective-permute-start(bf16[1,1,128,384]{3,2,1,0:T(8,128)(2,1)S(1)} %bitcast.216), channel_id=1, source_target_pairs={{0,16},{2,18},{4,20},{6,22},{8,24},{10,26},{12,28},{14,30},{16,0},... | collective-permute-start | bytes 294920 | tf_op jit(solution)/shard_map/ppermute | solution.py:185
  39.0 12.0 %collective-permute-start.5 = (bf16[2,256,1,384]{3,1,0,2:T(8,128)(2,1)S(1)}, bf16[2,256,1,384]{3,1,0,2:T(8,128)(2,1)S(1)}, u32[]{:S(2)}, u32[]{:S(2)}) collective-permute-start(bf16[2,256,1,384]{3,1,0,2:T(8,128)(2,1)S(1)} %bitcast.213), channel_id=1, source_target_pairs={{0,4},{2,6},{4,0},{6,2},{8,12},{10,14},{12,8},{14,10},{16,20},{18,... | collective-permute-start | bytes 1179656 | tf_op jit(solution)/shard_map/ppermute | solution.py:185
  40.1 10.3 %collective-permute-start.8 = (bf16[2,1,128,384]{3,2,1,0:T(8,128)(2,1)S(1)}, bf16[2,1,128,384]{3,2,1,0:T(8,128)(2,1)S(1)}, u32[]{:S(2)}, u32[]{:S(2)}) collective-permute-start(bf16[2,1,128,384]{3,2,1,0:T(8,128)(2,1)S(1)} %pad_maximum_fusion.10), channel_id=1, source_target_pairs={{0,8},{2,10},{4,12},{6,14},{8,0},{10,2},{12,4},{14,6},{16,24},{18,... | collective-permute-start | bytes 589832 | tf_op jit(solution)/shard_map/ppermute | solution.py:185
  50.4 10.3 %collective-permute-start.9 = (bf16[2,256,1,384]{3,1,0,2:T(8,128)(2,1)S(1)}, bf16[2,256,1,384]{3,1,0,2:T(8,128)(2,1)S(1)}, u32[]{:S(2)}, u32[]{:S(2)}) collective-permute-start(bf16[2,256,1,384]{3,1,0,2:T(8,128)(2,1)S(1)} %bitcast.214), channel_id=1, source_target_pairs={{0,4},{2,6},{4,0},{6,2},{8,12},{10,14},{12,8},{14,10},{16,20},{18,... | collective-permute-start | bytes 1179656 | tf_op jit(solution)/shard_map/ppermute | solution.py:185
  52.1 9.7 %copy-start.4 = (f32[1536]{0:T(1024)S(1)}, f32[1536]{0:T(1024)}, u32[]{:S(2)}) copy-start(f32[1536]{0:T(1024)} %param.18) | copy-start | bytes 18436
  52.1 9.7 %collective-permute-start.6 = (bf16[2,256,2,384]{3,1,0,2:T(8,128)(2,1)}, bf16[2,256,2,384]{3,1,0,2:T(8,128)(2,1)S(1)}, u32[]{:S(2)}, u32[]{:S(2)}) collective-permute-start(bf16[2,256,2,384]{3,1,0,2:T(8,128)(2,1)} %pad_maximum_fusion.1), channel_id=1, source_target_pairs={{0,2},{2,0},{4,6},{6,4},{8,10},{10,8},{12,14},{14,12},{16,18},{18,... | collective-permute-start | bytes 2359304 | tf_op jit(solution)/shard_map/ppermute | solution.py:185
  61.8 2.5 %collective-permute-start.10 = (bf16[2,256,2,384]{3,1,0,2:T(8,128)(2,1)}, bf16[2,256,2,384]{3,1,0,2:T(8,128)(2,1)S(1)}, u32[]{:S(2)}, u32[]{:S(2)}) collective-permute-start(bf16[2,256,2,384]{3,1,0,2:T(8,128)(2,1)} %pad_maximum_fusion.2), channel_id=1, source_target_pairs={{0,2},{2,0},{4,6},{6,4},{8,10},{10,8},{12,14},{14,12},{16,18},{18,... | collective-permute-start | bytes 2359304 | tf_op jit(solution)/shard_map/ppermute | solution.py:185
  68.4 3.5 %copy-start.1 = (bf16[2,256,4,2,384]{1,4,3,2,0:T(8,128)(2,1)S(1)}, bf16[2,256,4,2,384]{1,4,3,2,0:T(8,128)(2,1)}, u32[]{:S(2)}) copy-start(bf16[2,256,4,2,384]{1,4,3,2,0:T(8,128)(2,1)} %copy.69) | copy-start | bytes 9437188
  71.9 7.2 %slice-start = ((s8[4718592]{0:T(1024)(128)(4,1)}), s8[4194304]{0:T(1024)(128)(4,1)S(1)}, s32[]{:S(2)}) async-start(s8[4718592]{0:T(1024)(128)(4,1)} %bitcast.203), calls=%async_computation | async-start | bytes 8388608
  71.9 8.7 %slice-start.2 = ((s8[9437184]{0:T(1024)(128)(4,1)}), s8[4194304]{0:T(1024)(128)(4,1)S(1)}, s32[]{:S(2)}) async-start(s8[9437184]{0:T(1024)(128)(4,1)} %bitcast.230), calls=%async_computation.2 | async-start | bytes 8388608
  75.0 4.2 %slice-start.1 = ((s8[4718592]{0:T(1024)(128)(4,1)}), s8[524288]{0:T(1024)(128)(4,1)S(1)}, s32[]{:S(2)}) async-start(s8[4718592]{0:T(1024)(128)(4,1)} %bitcast.203), calls=%async_computation.1 | async-start | bytes 1048576
  75.0 5.6 %slice-start.3 = ((s8[9437184]{0:T(1024)(128)(4,1)}), s8[4194304]{0:T(1024)(128)(4,1)S(1)}, s32[]{:S(2)}) async-start(s8[9437184]{0:T(1024)(128)(4,1)} %bitcast.230), calls=%async_computation.3 | async-start | bytes 8388608
  79.2 1.5 slice-start.4
  84.4 9.2 %collective-permute-start.13 = (bf16[256,512]{1,0:T(8,128)(2,1)S(1)}, bf16[256,512]{1,0:T(8,128)(2,1)S(1)}, u32[]{:S(2)}, u32[]{:S(2)}) collective-permute-start(bf16[256,512]{1,0:T(8,128)(2,1)S(1)} %fusion.41), channel_id=1, source_target_pairs={{0,1},{1,0},{2,3},{3,2},{4,5},{5,4},{6,7},{7,6},{8,9},{9,8},{10,11... | collective-permute-start | bytes 786440 | tf_op jit(solution)/shard_map/ppermute | solution.py:181
  85.9 30.1 %collective-permute-start.12 = (bf16[256,768]{1,0:T(8,128)(2,1)S(1)}, bf16[256,768]{1,0:T(8,128)(2,1)S(1)}, u32[]{:S(2)}, u32[]{:S(2)}) collective-permute-start(bf16[256,768]{1,0:T(8,128)(2,1)S(1)} %fusion.32), channel_id=1, source_target_pairs={{0,1},{1,0},{2,3},{3,2},{4,5},{5,4},{6,7},{7,6},{8,9},{9,8},{10,11... | collective-permute-start | bytes 1179656 | tf_op jit(solution)/shard_map/ppermute | solution.py:181
  86.5 32.8 %collective-permute-start.11 = (bf16[256,512]{1,0:T(8,128)(2,1)}, bf16[256,512]{1,0:T(8,128)(2,1)}, u32[]{:S(2)}, u32[]{:S(2)}) collective-permute-start(bf16[256,512]{1,0:T(8,128)(2,1)} %fusion.36), channel_id=1, source_target_pairs={{0,1},{1,0},{2,3},{3,2},{4,5},{5,4},{6,7},{7,6},{8,9},{9,8},{10,11... | collective-permute-start | bytes 786440 | tf_op jit(solution)/shard_map/ppermute | solution.py:181
  88.0 25.3 %collective-permute-start.14 = (bf16[256,512]{1,0:T(8,128)(2,1)S(1)}, bf16[256,512]{1,0:T(8,128)(2,1)S(1)}, u32[]{:S(2)}, u32[]{:S(2)}) collective-permute-start(bf16[256,512]{1,0:T(8,128)(2,1)S(1)} %fusion.46), channel_id=1, source_target_pairs={{0,1},{1,0},{2,3},{3,2},{4,5},{5,4},{6,7},{7,6},{8,9},{9,8},{10,11... | collective-permute-start | bytes 786440 | tf_op jit(solution)/shard_map/ppermute | solution.py:181
  95.5 36.9 %collective-permute-start.19 = (bf16[256,512]{1,0:T(8,128)(2,1)}, bf16[256,512]{1,0:T(8,128)(2,1)S(1)}, u32[]{:S(2)}, u32[]{:S(2)}) collective-permute-start(bf16[256,512]{1,0:T(8,128)(2,1)} %fusion.65), channel_id=1, source_target_pairs={{0,1},{1,0},{2,3},{3,2},{4,5},{5,4},{6,7},{7,6},{8,9},{9,8},{10,11... | collective-permute-start | bytes 786440 | tf_op jit(solution)/shard_map/ppermute | solution.py:181
  114.5 18.6 %collective-permute-start.21 = (bf16[256,512]{1,0:T(8,128)(2,1)S(1)}, bf16[256,512]{1,0:T(8,128)(2,1)S(1)}, u32[]{:S(2)}, u32[]{:S(2)}) collective-permute-start(bf16[256,512]{1,0:T(8,128)(2,1)S(1)} %fusion.71), channel_id=1, source_target_pairs={{0,1},{1,0},{2,3},{3,2},{4,5},{5,4},{6,7},{7,6},{8,9},{9,8},{10,11... | collective-permute-start | bytes 786440 | tf_op jit(solution)/shard_map/ppermute | solution.py:181
  116.1 1.6 copy-start.5
  116.1 1.6 copy-start.6
  121.4 11.5 %collective-permute-start.20 = (bf16[256,512]{1,0:T(8,128)(2,1)S(1)}, bf16[256,512]{1,0:T(8,128)(2,1)S(1)}, u32[]{:S(2)}, u32[]{:S(2)}) collective-permute-start(bf16[256,512]{1,0:T(8,128)(2,1)S(1)} %fusion.68), channel_id=1, source_target_pairs={{0,1},{1,0},{2,3},{3,2},{4,5},{5,4},{6,7},{7,6},{8,9},{9,8},{10,11... | collective-permute-start | bytes 786440 | tf_op jit(solution)/shard_map/ppermute | solution.py:181
  125.9 5.5 %copy-start = (bf16[2,128,3072]{2,1,0:T(8,128)(2,1)S(1)}, bf16[2,128,3072]{2,1,0:T(8,128)(2,1)}, u32[]{:S(2)}) copy-start(bf16[2,128,3072]{2,1,0:T(8,128)(2,1)} %param.21) | copy-start | bytes 4718596
  125.9 7.2 %slice-start.5 = ((s8[9437184]{0:T(1024)(128)(4,1)}), s8[4194304]{0:T(1024)(128)(4,1)S(1)}, s32[]{:S(2)}) async-start(s8[9437184]{0:T(1024)(128)(4,1)} %bitcast.232), calls=%async_computation.5 | async-start | bytes 8388608
  125.9 7.2 %slice-start.6 = ((s8[9437184]{0:T(1024)(128)(4,1)}), s8[4194304]{0:T(1024)(128)(4,1)S(1)}, s32[]{:S(2)}) async-start(s8[9437184]{0:T(1024)(128)(4,1)} %bitcast.232), calls=%async_computation.6 | async-start | bytes 8388608
  129.8 6.0 %collective-permute-start.18 = (bf16[256,256]{0,1:T(8,128)(2,1)S(1)}, bf16[256,256]{0,1:T(8,128)(2,1)S(1)}, u32[]{:S(2)}, u32[]{:S(2)}) collective-permute-start(bf16[256,256]{0,1:T(8,128)(2,1)S(1)} %bitcast.223), channel_id=1, source_target_pairs={{0,1},{1,0},{2,3},{3,2},{4,5},{5,4},{6,7},{7,6},{8,9},{9,8},{10,11... | collective-permute-start | bytes 393224 | tf_op jit(solution)/shard_map/ppermute | solution.py:181
  131.4 1.7 slice-start.7
  131.9 5.6 %collective-permute-start.15 = (bf16[2,2,32,1536]{3,2,1,0:T(8,128)(2,1)S(1)}, bf16[2,2,32,1536]{3,2,1,0:T(8,128)(2,1)S(1)}, u32[]{:S(2)}, u32[]{:S(2)}) collective-permute-start(bf16[2,2,32,1536]{3,2,1,0:T(8,128)(2,1)S(1)} %fusion.98), channel_id=1, source_target_pairs={{0,2},{2,0},{4,6},{6,4},{8,10},{10,8},{12,14},{14,12},{16,18},{18,... | collective-permute-start | bytes 1179656 | tf_op jit(solution)/shard_map/ppermute | solution.py:185
  132.4 5.8 %collective-permute-start.26 = (bf16[2,2,32,1536]{3,2,1,0:T(8,128)(2,1)S(1)}, bf16[2,2,32,1536]{3,2,1,0:T(8,128)(2,1)S(1)}, u32[]{:S(2)}, u32[]{:S(2)}) collective-permute-start(bf16[2,2,32,1536]{3,2,1,0:T(8,128)(2,1)S(1)} %fusion.100), channel_id=1, source_target_pairs={{0,2},{2,0},{4,6},{6,4},{8,10},{10,8},{12,14},{14,12},{16,18},{18,... | collective-permute-start | bytes 1179656 | tf_op jit(solution)/shard_map/ppermute | solution.py:185
  136.3 12.8 %collective-permute-start.22 = (bf16[2,2,32,1536]{3,2,1,0:T(8,128)(2,1)S(1)}, bf16[2,2,32,1536]{3,2,1,0:T(8,128)(2,1)S(1)}, u32[]{:S(2)}, u32[]{:S(2)}) collective-permute-start(bf16[2,2,32,1536]{3,2,1,0:T(8,128)(2,1)S(1)} %fusion.99), channel_id=1, source_target_pairs={{0,2},{2,0},{4,6},{6,4},{8,10},{10,8},{12,14},{14,12},{16,18},{18,... | collective-permute-start | bytes 1179656 | tf_op jit(solution)/shard_map/ppermute | solution.py:185
  136.9 13.0 %collective-permute-start.29 = (bf16[2,2,32,1536]{3,2,1,0:T(8,128)(2,1)S(1)}, bf16[2,2,32,1536]{3,2,1,0:T(8,128)(2,1)S(1)}, u32[]{:S(2)}, u32[]{:S(2)}) collective-permute-start(bf16[2,2,32,1536]{3,2,1,0:T(8,128)(2,1)S(1)} %fusion.101), channel_id=1, source_target_pairs={{0,2},{2,0},{4,6},{6,4},{8,10},{10,8},{12,14},{14,12},{16,18},{18,... | collective-permute-start | bytes 1179656 | tf_op jit(solution)/shard_map/ppermute | solution.py:185
  137.6 7.8 %collective-permute-start.16 = (bf16[2,32,1536]{2,1,0:T(8,128)(2,1)S(1)}, bf16[2,32,1536]{2,1,0:T(8,128)(2,1)S(1)}, u32[]{:S(2)}, u32[]{:S(2)}) collective-permute-start(bf16[2,32,1536]{2,1,0:T(8,128)(2,1)S(1)} %fusion.108), channel_id=1, source_target_pairs={{0,4},{2,6},{4,0},{6,2},{8,12},{10,14},{12,8},{14,10},{16,20},{18,... | collective-permute-start | bytes 589832 | tf_op jit(solution)/shard_map/ppermute | solution.py:185
  138.3 10.3 %collective-permute-start.27 = (bf16[2,32,1536]{2,1,0:T(8,128)(2,1)S(1)}, bf16[2,32,1536]{2,1,0:T(8,128)(2,1)S(1)}, u32[]{:S(2)}, u32[]{:S(2)}) collective-permute-start(bf16[2,32,1536]{2,1,0:T(8,128)(2,1)S(1)} %fusion.110), channel_id=1, source_target_pairs={{0,4},{2,6},{4,0},{6,2},{8,12},{10,14},{12,8},{14,10},{16,20},{18,... | collective-permute-start | bytes 589832 | tf_op jit(solution)/shard_map/ppermute | solution.py:185
  145.5 15.6 %collective-permute-start.17 = (bf16[32,1536]{1,0:T(8,128)(2,1)S(1)}, bf16[32,1536]{1,0:T(8,128)(2,1)S(1)}, u32[]{:S(2)}, u32[]{:S(2)}) collective-permute-start(bf16[32,1536]{1,0:T(8,128)(2,1)S(1)} %fusion.128), channel_id=1, source_target_pairs={{0,8},{2,10},{4,12},{6,14},{8,0},{10,2},{12,4},{14,6},{16,24},{18,... | collective-permute-start | bytes 294920 | tf_op jit(solution)/shard_map/ppermute | solution.py:185
  148.7 16.1 %collective-permute-start.28 = (bf16[32,1536]{1,0:T(8,128)(2,1)S(1)}, bf16[32,1536]{1,0:T(8,128)(2,1)S(1)}, u32[]{:S(2)}, u32[]{:S(2)}) collective-permute-start(bf16[32,1536]{1,0:T(8,128)(2,1)S(1)} %fusion.130), channel_id=1, source_target_pairs={{0,8},{2,10},{4,12},{6,14},{8,0},{10,2},{12,4},{14,6},{16,24},{18,... | collective-permute-start | bytes 294920 | tf_op jit(solution)/shard_map/ppermute | solution.py:185
  149.3 7.9 %collective-permute-start.23 = (bf16[2,32,1536]{2,1,0:T(8,128)(2,1)S(1)}, bf16[2,32,1536]{2,1,0:T(8,128)(2,1)S(1)}, u32[]{:S(2)}, u32[]{:S(2)}) collective-permute-start(bf16[2,32,1536]{2,1,0:T(8,128)(2,1)S(1)} %fusion.109), channel_id=1, source_target_pairs={{0,4},{2,6},{4,0},{6,2},{8,12},{10,14},{12,8},{14,10},{16,20},{18,... | collective-permute-start | bytes 589832 | tf_op jit(solution)/shard_map/ppermute | solution.py:185
  150.0 9.3 %collective-permute-start.30 = (bf16[2,32,1536]{2,1,0:T(8,128)(2,1)S(1)}, bf16[2,32,1536]{2,1,0:T(8,128)(2,1)S(1)}, u32[]{:S(2)}, u32[]{:S(2)}) collective-permute-start(bf16[2,32,1536]{2,1,0:T(8,128)(2,1)S(1)} %fusion.111), channel_id=1, source_target_pairs={{0,4},{2,6},{4,0},{6,2},{8,12},{10,14},{12,8},{14,10},{16,20},{18,... | collective-permute-start | bytes 589832 | tf_op jit(solution)/shard_map/ppermute | solution.py:185
  157.2 4.9 %collective-permute-start.24 = (bf16[32,1536]{1,0:T(8,128)(2,1)S(1)}, bf16[32,1536]{1,0:T(8,128)(2,1)S(1)}, u32[]{:S(2)}, u32[]{:S(2)}) collective-permute-start(bf16[32,1536]{1,0:T(8,128)(2,1)S(1)} %fusion.129), channel_id=1, source_target_pairs={{0,8},{2,10},{4,12},{6,14},{8,0},{10,2},{12,4},{14,6},{16,24},{18,... | collective-permute-start | bytes 294920 | tf_op jit(solution)/shard_map/ppermute | solution.py:185
  159.3 11.3 %copy-start.2 = (bf16[32,3072]{1,0:T(8,128)(2,1)S(1)}, bf16[32,3072]{1,0:T(8,128)(2,1)}, u32[]{:S(2)}) copy-start(bf16[32,3072]{1,0:T(8,128)(2,1)} %param.12) | copy-start | bytes 589828
  159.3 11.3 %copy-start.3 = (f32[3072]{0:T(1024)S(1)}, f32[3072]{0:T(1024)}, u32[]{:S(2)}) copy-start(f32[3072]{0:T(1024)} %param.23) | copy-start | bytes 36868
  159.4 5.5 %collective-permute-start.31 = (bf16[32,1536]{1,0:T(8,128)(2,1)S(1)}, bf16[32,1536]{1,0:T(8,128)(2,1)S(1)}, u32[]{:S(2)}, u32[]{:S(2)}) collective-permute-start(bf16[32,1536]{1,0:T(8,128)(2,1)S(1)} %fusion.131), channel_id=1, source_target_pairs={{0,8},{2,10},{4,12},{6,14},{8,0},{10,2},{12,4},{14,6},{16,24},{18,... | collective-permute-start | bytes 294920 | tf_op jit(solution)/shard_map/ppermute | solution.py:185
  162.1 7.4 %collective-permute-start.25 = (bf16[32,1536]{1,0:T(8,128)(2,1)S(1)}, bf16[32,1536]{1,0:T(8,128)(2,1)S(1)}, u32[]{:S(2)}, u32[]{:S(2)}) collective-permute-start(bf16[32,1536]{1,0:T(8,128)(2,1)S(1)} %select_convert_fusion.1), channel_id=1, source_target_pairs={{0,16},{2,18},{4,20},{6,22},{8,24},{10,26},{12,28},{14,30},{16,0},... | collective-permute-start | bytes 294920 | tf_op jit(solution)/shard_map/ppermute | solution.py:185
  164.9 5.7 %collective-permute-start.32 = (bf16[32,1536]{1,0:T(8,128)(2,1)S(1)}, bf16[32,1536]{1,0:T(8,128)(2,1)S(1)}, u32[]{:S(2)}, u32[]{:S(2)}) collective-permute-start(bf16[32,1536]{1,0:T(8,128)(2,1)S(1)} %select_convert_fusion), channel_id=1, source_target_pairs={{0,16},{2,18},{4,20},{6,22},{8,24},{10,26},{12,28},{14,30},{16,0},... | collective-permute-start | bytes 294920 | tf_op jit(solution)/shard_map/ppermute | solution.py:185
